TPU v7x, 32 devices: a whole 2x2x4 slice. The times are simulated.
32 devices in a mesh: lon: 8 (over z, y), lat: 4 (over x, core).
Axes of the slice: x: 2, y: 2, z: 4, core: 2. Of those that a mesh axis runs over, the one named last changes fastest.
Arguments:
- tracers: float32 [2, 4, 64, 1024], P(None, None, 'lat', 'lon'), may hold values from -6 to 6
- land_mask: int32 [64, 1024], P('lat', 'lon'), may hold values 0 or 1
- level_counts: int32 [64, 1024], P('lat', 'lon'), may hold values from 1 to 4
- fold_partner: int32 [1024], P('lon'), may hold values from 0 to 1023, as said below
- cotangent: float32 [2, 4, 64, 1024], P(None, None, 'lat', 'lon'), may hold values from -6 to 6
- w_first: float32 [6, 128], replicated, may hold values from -2.5 to 2.5
- b_first: float32 [128], replicated, may hold values from -3 to 3
- w_second: float32 [128, 128], replicated, may hold values from -0.5 to 0.5
- b_second: float32 [128], replicated, may hold values from -3 to 3
- w_head: float32 [128], replicated, may hold values from -0.5 to 0.5
- b_head: float32 [1], replicated, may hold values from -3 to 3
Outputs:
- tracers_out: float32 [2, 4, 64, 1024], P(None, None, 'lat', 'lon')
- tracer_grad: float32 [2, 4, 64, 1024], P(None, None, 'lat', 'lon')
- w_first_grad: float32 [6, 128], replicated
- w_second_grad: float32 [128, 128], replicated
- w_head_grad: float32 [128], replicated
Inputs may be any that keep to these rules, and one draw needn't show every extreme that they name: fold_partner[x] = (s - x) mod 1024 for one odd whole number s of the draw: the mirror about the fold line, so fold_partner[fold_partner[x]] = x and fold_partner[x] != x.
All inputs are finite; a program needn't handle non-finite values. No bound on the sum of `land_mask` on one device may be relied on, other than what follows from the above.
Results may differ from a plain program's by a relative error of at most 0.0003.
Values sent between devices are 32-bit elements; how exact they have to be, the bound alone decides.
No kernel may reach another device: no remote copies, remote signals or barrier semaphores. Data moves between devices by JAX's collectives and lax.ppermute only.
A program may use at most 128 MiB of HBM per device.

v0:
```python
import functools
import math

import jax
import jax.numpy as jnp
from jax import lax
from jax.experimental import pallas as pl
from jax.experimental.pallas import tpu as pltpu
from jax.sharding import PartitionSpec as P

KMAX = 0.24
DEPTH = 4
HID = 128
LANES = 128
HALO = 3
SLOT = 2 * HALO
F32 = jnp.float32
BF16 = jnp.bfloat16


def split(x):
    high = x.astype(BF16)
    low = (x - high.astype(F32)).astype(BF16)
    return high, low


def iota(shape, dim):
    return lax.broadcasted_iota(jnp.int32, shape, dim)


def pack_rows_kernel(rows, tracer, cot, land, levels, south, north):
    depth = (land[...] * levels[...]).astype(F32)
    for out, first in ((south, 0), (north, rows - HALO)):
        for j in range(HALO):
            out[8 * j : 8 * j + 8, :] = tracer[pl.ds(first + j, 8, stride=rows), :]
        skip = 0 if first == 0 else 1
        for j in range(2):
            out[24 + 8 * j : 32 + 8 * j, :] = cot[pl.ds(first + skip + j, 8, stride=rows), :]
        out[40:48, :] = jnp.concatenate(
            [depth[first : first + HALO], jnp.zeros((8 - HALO, LANES), F32)], 0
        )


def weights_kernel(w1, b1, w2, b2, wh, a1_out, w2t_out, w2_out, t1_out, col_out):
    first = w1[...]
    bias_high, bias_low = split(b1[...])
    row = iota((16, LANES), 0)
    pad_row = iota((16, LANES), 0)
    for k in range(DEPTH):
        block = jnp.zeros((16, LANES), F32)
        for t in range(2):
            block = jnp.where(row == t * 4 + k, first[t : t + 1], block)
            if k >= 1:
                block = jnp.where(row == 8 + t * 4 + k - 1, -first[2 + t : 3 + t], block)
            block = jnp.where(row == 8 + t * 4 + k, first[4 + t : 5 + t], block)
        high, low = split(block)
        high32, low32 = high.astype(F32), low.astype(F32)
        tail = jnp.where(
            pad_row == 0,
            bias_high.astype(F32),
            jnp.where(pad_row == 1, bias_low.astype(F32), 0.0),
        )
        tall = jnp.concatenate([high32, high32, low32, tail, jnp.zeros((64, LANES), F32)], 0)
        a1_out[k * HID : (k + 1) * HID, :] = jnp.transpose(tall)[:, :64].astype(BF16)
        t1_out[k * 32 : k * 32 + 16, :] = jnp.concatenate([high, high], 1)
        t1_out[k * 32 + 16 : k * 32 + 32, :] = jnp.concatenate([low, jnp.zeros_like(low)], 1)
    second = w2[...]
    for out, matrix in ((w2_out, second), (w2t_out, jnp.transpose(second))):
        high, low = split(matrix)
        out[0:HID, :] = jnp.concatenate([high, high], 1)
        out[HID : 2 * HID, :] = jnp.concatenate([low, low], 1)
    for place, vector in ((0, b2), (HID, wh)):
        column = jnp.transpose(jnp.broadcast_to(vector[...], (HID, LANES)))
        col_out[place : place + HID, :] = jnp.concatenate([column, column], 1)


def assemble_kernel(
    rows, partner, from_north, from_south, fold_near, fold_far, tracer, cot, land, levels, ext, packed
):
    lane = iota((8, LANES), 1)
    at_top = lax.axis_index("lat") == lax.axis_size("lat") - 1
    offset = jnp.bitwise_and(partner[0], LANES - 1)
    source = jnp.bitwise_and(offset - lane, LANES - 1)

    def mirrored(place):
        both = jnp.where(
            lane <= offset, fold_near[place : place + 8, :], fold_far[place : place + 8, :]
        )
        return jnp.take_along_axis(both, source, axis=1)

    def north(plain, folded):
        return jnp.where(at_top, mirrored(folded), from_north[plain : plain + 8, :])

    zero = jnp.zeros((8, LANES), F32)

    def spread(tile, j):
        return jnp.broadcast_to(tile[j : j + 1], (8, LANES))

    depth_here = (land[...] * levels[...]).astype(F32)
    depth_south = from_south[40:48, :]
    depth_north = from_north[40:48, :]
    depth_fold = mirrored(40)
    total = rows + 2 * HALO
    tiles = []
    for i in range(total):
        r = i - HALO
        if r < 0:
            tile_c = from_south[8 * i : 8 * i + 8, :]
            tile_l = from_south[24 + 8 * (i - 1) : 32 + 8 * (i - 1), :] if i >= 1 else zero
            tile_n = spread(depth_south, i)
        elif r < rows:
            tile_c = tracer[pl.ds(r, 8, stride=rows), :]
            tile_l = cot[pl.ds(r, 8, stride=rows), :]
            tile_n = spread(depth_here, r)
        else:
            j = r - rows
            tile_c = north(8 * j, 8 * (2 - j))
            tile_l = north(24 + 8 * j, 24 + 8 * (1 - j)) if j < 2 else zero
            tile_n = jnp.where(at_top, spread(depth_fold, 2 - j), spread(depth_north, j))
        tiles.append((tile_c, tile_l, tile_n))
        for part, tile in enumerate(tiles[-1]):
            ext[24 * i + 8 * part : 24 * i + 8 * part + 8, :] = tile
    for part in range(3):
        acc = zero
        for slot in range(rows + 4):
            moved = pltpu.roll(tiles[slot + 1][part], SLOT * slot + HALO, 1)
            inside = (lane >= SLOT * slot) & (lane < SLOT * slot + SLOT)
            acc = jnp.where(inside, moved, acc)
        packed[8 * part : 8 * part + 8, :] = acc


def steps_kernel(
    rows,
    head_bias,
    ext,
    west_in,
    east_in,
    a1,
    w2t,
    w2,
    t1,
    cols,
    out_tracer,
    out_grad,
    out_sums,
    c_tiles0,
    c_tiles1,
    wv_tiles,
    wet_tiles,
    kappa_tiles,
    slope0,
    slope1,
    d3_tiles,
    bar_tiles,
    x0,
    x1,
    h1b0,
    h1b1,
    h1f0,
    h1f1,
    h2f0,
    h2f1,
    acc_w2,
    acc_a1,
    acc_head,
):
    total = rows + 2 * HALO
    lane = iota((8, LANES), 1)
    level = jnp.bitwise_and(iota((8, LANES), 0), DEPTH - 1)
    level_wide = jnp.bitwise_and(iota((8, 2 * LANES), 0), DEPTH - 1)
    zero = jnp.zeros((8, LANES), F32)
    side_tile = rows
    tile_of = {i: i - HALO for i in range(HALO, rows + HALO)}
    place = rows + 1
    for ring in (1, 2, 3):
        tile_of[HALO - ring] = place
        tile_of[rows + HALO - 1 + ring] = place + 1
        place += 2
    n_tiles = place + (place % 2)
    slots = range(1, rows + 5)

    def east(main, side):
        return (
            pltpu.roll(jnp.where(lane == 0, side, main), LANES - 1, 1),
            pltpu.roll(jnp.where(lane == 0, main, side), LANES - 1, 1),
        )

    def from_west(main, side):
        return (
            pltpu.roll(jnp.where(lane == LANES - 1, side, main), 1, 1),
            pltpu.roll(jnp.where(lane == LANES - 1, main, side), 1, 1),
        )

    def from_west_main(main, side):
        return pltpu.roll(jnp.where(lane == LANES - 1, side, main), 1, 1)

    def unpack(tile, i):
        return pltpu.roll(tile, LANES - (SLOT * (i - 1) + HALO), 1)

    def pack(tiles):
        acc = zero
        for i, tile in tiles.items():
            slot = i - 1
            moved = pltpu.roll(tile, SLOT * slot + HALO, 1)
            inside = (lane >= SLOT * slot) & (lane < SLOT * slot + SLOT)
            acc = jnp.where(inside, moved, acc)
        return acc

    def both(x):
        return x + pltpu.roll(x, 4, 0)

    third = lax.rem(lane, SLOT)
    from_left = third < HALO
    side_c_packed = jnp.where(from_left, west_in[0:8, :], east_in[0:8, :])
    side_l_packed = jnp.where(from_left, west_in[8:16, :], east_in[8:16, :])
    side_n_packed = jnp.where(from_left, west_in[16:24, :], east_in[16:24, :])
    side_lanes = (lane < HALO) | (lane >= LANES - HALO)

    def wet_of(depth):
        return jnp.where(depth > level.astype(F32), 1.0, 0.0)

    def vertical_of(depth):
        inside = (depth > (level + 1).astype(F32)) & (level < DEPTH - 1)
        return jnp.where(inside, 1.0, 0.0)

    c0, wet = {}, {}
    for i in range(total):
        depth = ext[24 * i + 16 : 24 * i + 24, :]
        main_c = ext[24 * i : 24 * i + 8, :]
        main_w = wet_of(depth)
        if i in slots:
            side_c = unpack(side_c_packed, i)
            side_w = jnp.where(side_lanes, wet_of(unpack(side_n_packed, i)), 0.0)
        else:
            side_c, side_w = zero, zero
        c0[i] = (main_c, side_c)
        wet[i] = (main_w, side_w)
        c_tiles0[tile_of[i]] = main_c
        wet_tiles[tile_of[i]] = main_w
        wv_tiles[tile_of[i]] = vertical_of(depth)
    c_tiles0[side_tile] = side_c_packed
    wet_tiles[side_tile] = wet_of(side_n_packed)
    wv_tiles[side_tile] = vertical_of(side_n_packed)
    for tile in range(place, n_tiles):
        c_tiles0[tile] = zero
        wet_tiles[tile] = zero
        wv_tiles[tile] = zero

    def closure(pairs, c_tiles, slope, xs, h1b, h1f, h2f):
        def body(p, carry):
            pieces = []
            for a in range(2):
                c = c_tiles[2 * p + a]
                v = (pltpu.roll(c, 7, 0) - c) * wv_tiles[2 * p + a]
                pieces.append(jnp.concatenate([c, v], 0))
            high, low = split(jnp.concatenate(pieces, 1))
            x = jnp.concatenate([high, low, high, jnp.ones((16, 2 * LANES), BF16)], 0)
            xs[p] = x
            out = jnp.zeros((8, 2 * LANES), F32)
            for k in range(DEPTH):
                h1 = jnp.tanh(
                    jnp.dot(a1[k * HID : (k + 1) * HID, :], x, preferred_element_type=F32)
                )
                h1f[p, k] = h1
                pair = jnp.concatenate(split(h1), 0)
                h1b[p, k] = pair
                z = jnp.dot(w2t[...], pair, preferred_element_type=F32)
                h2 = jnp.tanh(z[:HID] + z[HID:] + cols[0:HID, :])
                h2f[p, k] = h2
                head = jnp.sum(h2 * cols[HID : 2 * HID, :], 0, keepdims=True)
                out = jnp.where(level_wide == k, head, out)
            sig = jax.nn.sigmoid(out + head_bias[0])
            for a in range(2):
                part = sig[:, a * LANES : (a + 1) * LANES]
                kappa = KMAX * part * wet_tiles[2 * p + a]
                kappa_tiles[2 * p + a] = kappa
                slope[2 * p + a] = kappa * (1.0 - part)
            return carry

        lax.fori_loop(0, pairs, body, 0)

    def edge_masks(i):
        east_w = east(*wet[i])
        return tuple(0.5 * a * b for a, b in zip(wet[i], east_w))

    def north_mask(i):
        return tuple(0.5 * a * b for a, b in zip(wet[i], wet[i + 1]))

    def kappas(lo, hi):
        packed = kappa_tiles[side_tile]
        out = {}
        for i in range(lo, hi + 1):
            side = unpack(packed, i) if i in slots else zero
            out[i] = (kappa_tiles[tile_of[i]], side)
        return out

    def coefficients(kappa, lo, hi):
        ce, cn = {}, {}
        for i in range(lo, hi + 1):
            ke = east(*kappa[i])
            ce[i] = tuple(m * (a + b) for m, a, b in zip(edge_masks(i), kappa[i], ke))
        for i in range(lo - 1, hi + 1):
            cn[i] = tuple(
                m * (a + b) for m, a, b in zip(north_mask(i), kappa[i], kappa[i + 1])
            )
        return ce, cn

    def diffs(field, lo, hi):
        de, dn = {}, {}
        for i in range(lo, hi + 1):
            fe = east(*field[i])
            de[i] = tuple(b - a for a, b in zip(field[i], fe))
        for i in range(lo - 1, hi + 1):
            dn[i] = tuple(b - a for a, b in zip(field[i], field[i + 1]))
        return de, dn

    def diffuse(field, ce, cn, de, dn, lo, hi):
        out = {}
        flux_n = {i: tuple(c * d for c, d in zip(cn[i], dn[i])) for i in range(lo - 1, hi + 1)}
        for i in range(lo, hi + 1):
            fe = tuple(c * d for c, d in zip(ce[i], de[i]))
            fw = from_west(*fe)
            out[i] = tuple(
                f + ((a - b) + (c - d))
                for f, a, b, c, d in zip(field[i], fe, fw, flux_n[i], flux_n[i - 1])
            )
        return out

    def kappa_bars(de, dn, le, ln, lo, hi):
        out = {}
        gn = {}
        for i in range(lo - 1, hi + 1):
            gn[i] = tuple(-m * a * b for m, a, b in zip(north_mask(i), dn[i], ln[i]))
        for i in range(lo, hi + 1):
            ge = tuple(-m * a * b for m, a, b in zip(edge_masks(i), de[i], le[i]))
            gw = from_west(*ge)
            out[i] = tuple(
                both((a + b) + (c + d)) for a, b, c, d in zip(ge, gw, gn[i], gn[i - 1])
            )
        return out

    def closure_back(start, pairs, with_sums, slope, xs, h1b, h1f, h2f):
        def body(step, carry):
            p = start + step
            d3 = jnp.concatenate(
                [d3_tiles[2 * p + a] * slope[2 * p + a] for a in range(2)], 1
            )
            bar = jnp.zeros((32, 2 * LANES), F32)
            sum_w2 = None
            sum_head = None
            for k in range(DEPTH):
                h2 = h2f[p, k]
                row = d3[k : k + 1]
                d2 = (cols[HID : 2 * HID, :] * row) * (1.0 - h2 * h2)
                d2b = jnp.concatenate(split(d2), 0)
                e = jnp.dot(w2[...], d2b, preferred_element_type=F32)
                h1 = h1f[p, k]
                d1 = (e[:HID] + e[HID:]) * (1.0 - h1 * h1)
                d1b = jnp.concatenate(split(d1), 0)
                bar = bar + jnp.dot(
                    t1[k * 32 : (k + 1) * 32, :], d1b, preferred_element_type=F32
                )
                if with_sums:
                    part = h2 * row
                    sum_head = part if sum_head is None else sum_head + part
                    outer = lax.dot_general(
                        h1b[p, k], d2b, (((1,), (1,)), ((), ())), preferred_element_type=F32
                    )
                    sum_w2 = outer if sum_w2 is None else sum_w2 + outer
                    acc_a1[k] += lax.dot_general(
                        d1b, xs[p, 0:32, :], (((1,), (1,)), ((), ())), preferred_element_type=F32
                    )
            if with_sums:
                acc_w2[...] += sum_w2
                acc_head[...] += sum_head
            for a in range(2):
                part = bar[:, a * LANES : (a + 1) * LANES]
                part = part[:16] + part[16:]
                v = part[8:] * wv_tiles[2 * p + a]
                bar_tiles[2 * p + a] = part[:8] - v + pltpu.roll(v, 1, 0)
            return carry

        lax.fori_loop(0, pairs, body, 0)

    low, high = HALO, rows + HALO - 1
    closure(n_tiles // 2, c_tiles0, slope0, x0, h1b0, h1f0, h2f0)
    kappa0 = kappas(0, total - 1)
    ce0, cn0 = coefficients(kappa0, low - 2, high + 2)
    de0, dn0 = diffs(c0, low - 2, high + 2)
    c1 = diffuse(c0, ce0, cn0, de0, dn0, low - 2, high + 2)
    for i in range(low - 2, high + 3):
        c_tiles1[tile_of[i]] = c1[i][0]
    c_tiles1[side_tile] = pack({i: c1[i][1] for i in range(low - 2, high + 3)})
    tiles1 = rows + 5
    for tile in range(tiles1, n_tiles):
        c_tiles1[tile] = zero
    closure((tiles1 + 1) // 2, c_tiles1, slope1, x1, h1b1, h1f1, h2f1)
    kappa1 = kappas(low - 2, high + 2)
    ce1, cn1 = coefficients(kappa1, low - 1, high + 1)
    de1, dn1 = diffs(c1, low - 1, high + 1)
    c2 = diffuse(c1, ce1, cn1, de1, dn1, low, high)
    for i in range(low, high + 1):
        out_tracer[pl.ds(i - low, 8, stride=rows), :] = c2[i][0]
    lam2 = {}
    for i in range(low - 2, high + 3):
        lam2[i] = (ext[24 * i + 8 : 24 * i + 16, :], unpack(side_l_packed, i))
    le, ln = diffs(lam2, low - 1, high + 1)
    direct = diffuse(lam2, ce1, cn1, le, ln, low - 1, high + 1)
    bars = kappa_bars(de1, dn1, le, ln, low - 1, high + 1)
    for i in range(low - 1, high + 2):
        d3_tiles[tile_of[i]] = bars[i][0]
    d3_tiles[side_tile] = pack({i: bars[i][1] for i in range(low, high + 1)})
    d3_tiles[rows + 3] = zero
    acc_w2[...] = jnp.zeros_like(acc_w2)
    acc_a1[...] = jnp.zeros_like(acc_a1)
    acc_head[...] = jnp.zeros_like(acc_head)
    closure_back(0, rows // 2, True, slope1, x1, h1b1, h1f1, h2f1)
    closure_back(rows // 2, 2, False, slope1, x1, h1b1, h1f1, h2f1)
    side_bar = bar_tiles[side_tile]
    lam1 = {}
    for i in range(low - 1, high + 2):
        main = direct[i][0] + bar_tiles[tile_of[i]]
        side = direct[i][1] + unpack(side_bar, i)
        lam1[i] = (main, side)
    le, ln = diffs(lam1, low, high)
    direct = diffuse(lam1, ce0, cn0, le, ln, low, high)
    bars = kappa_bars(de0, dn0, le, ln, low, high)
    for i in range(low, high + 1):
        d3_tiles[tile_of[i]] = bars[i][0]
    closure_back(0, rows // 2, True, slope0, x0, h1b0, h1f0, h2f0)
    for i in range(low, high + 1):
        out_grad[pl.ds(i - low, 8, stride=rows), :] = direct[i][0] + bar_tiles[tile_of[i]]
    out_sums[0:HID, :] = (acc_w2[:HID, :HID] + acc_w2[HID:, HID:]) + (
        acc_w2[:HID, HID:] + acc_w2[HID:, :HID]
    )
    first = [None] * 6

    def add(f, value):
        first[f] = value if first[f] is None else first[f] + value

    for k in range(DEPTH):
        cells = acc_a1[k]
        cells = cells[:HID] + cells[HID:]
        cells = jnp.concatenate([cells, jnp.zeros((HID, LANES - 32), F32)], 1)
        turned = jnp.transpose(cells)
        turned = turned[0:16] + turned[16:32]
        for t in range(2):
            add(t, turned[t * 4 + k : t * 4 + k + 1])
            if k >= 1:
                add(2 + t, -turned[8 + t * 4 + k - 1 : 8 + t * 4 + k])
            add(4 + t, turned[8 + t * 4 + k : 8 + t * 4 + k + 1])
    head = jnp.sum(jnp.transpose(acc_head[:, :LANES] + acc_head[:, LANES:]), 0, keepdims=True)
    out_sums[HID : HID + 8, :] = jnp.concatenate(first + [head, jnp.zeros_like(head)], 0)


def finish_kernel(scale, mine, other, w1_out, w2_out, wh_out):
    w2_out[...] = (mine[0:HID, :] + other[0:HID, :]) * scale
    rest = (mine[HID : HID + 8, :] + other[HID : HID + 8, :]) * scale
    w1_out[...] = rest[0:6]
    wh_out[...] = rest[6:7]


VMEM = pl.BlockSpec(memory_space=pltpu.VMEM)
SMEM = pl.BlockSpec(memory_space=pltpu.SMEM)


def call(kernel, outs, ins, scratch=(), limit=None, flops=1_000_000, size=1_000_000):
    return pl.pallas_call(
        kernel,
        out_shape=outs,
        in_specs=ins,
        out_specs=[VMEM] * len(outs),
        scratch_shapes=list(scratch),
        compiler_params=pltpu.CompilerParams(vmem_limit_bytes=limit),
        cost_estimate=pl.CostEstimate(flops=flops, bytes_accessed=size, transcendentals=0),
    )


def shape(*dims, dtype=F32):
    return jax.ShapeDtypeStruct(dims, dtype)


def per_device(
    tracers,
    land_mask,
    level_counts,
    fold_partner,
    cotangent,
    w_first,
    b_first,
    w_second,
    b_second,
    w_head,
    b_head,
):
    rows, cols = land_mask.shape
    n_lon, n_lat = lax.axis_size("lon"), lax.axis_size("lat")
    tracer2 = tracers.reshape(8 * rows, cols)
    cot2 = cotangent.reshape(8 * rows, cols)

    south, north = call(
        functools.partial(pack_rows_kernel, rows), [shape(48, LANES)] * 2, [VMEM] * 4
    )(tracer2, cot2, land_mask, level_counts)
    from_north = lax.ppermute(south, "lat", [(i + 1, i) for i in range(n_lat - 1)])
    from_south = lax.ppermute(north, "lat", [(i, i + 1) for i in range(n_lat - 1)])

    turn = lax.rem(fold_partner[0] // cols + lax.axis_index("lon"), n_lon)

    def across(j, rows_out):
        def pairs(add):
            return [
                (b * n_lat + n_lat - 1, ((j + add - b) % n_lon) * n_lat + n_lat - 1)
                for b in range(n_lon)
            ]

        return (
            lax.ppermute(rows_out, ("lon", "lat"), pairs(0)),
            lax.ppermute(rows_out, ("lon", "lat"), pairs(-1)),
        )

    fold_near, fold_far = lax.switch(
        turn, [functools.partial(across, j) for j in range(n_lon)], north
    )

    a1, w2t, w2, t1, cols_w = call(
        weights_kernel,
        [
            shape(DEPTH * HID, 64, dtype=BF16),
            shape(2 * HID, 2 * HID, dtype=BF16),
            shape(2 * HID, 2 * HID, dtype=BF16),
            shape(DEPTH * 32, 2 * HID, dtype=BF16),
            shape(2 * HID, 2 * LANES),
        ],
        [VMEM] * 5,
    )(w_first, b_first.reshape(1, HID), w_second, b_second.reshape(1, HID), w_head.reshape(1, HID))

    total = rows + 2 * HALO
    ext, packed = call(
        functools.partial(assemble_kernel, rows),
        [shape(24 * total, LANES), shape(24, LANES)],
        [SMEM] + [VMEM] * 8,
    )(
        fold_partner,
        from_north,
        from_south,
        fold_near,
        fold_far,
        tracer2,
        cot2,
        land_mask,
        level_counts,
    )
    from_west = lax.ppermute(packed, "lon", [(i, (i + 1) % n_lon) for i in range(n_lon)])
    from_east = lax.ppermute(packed, "lon", [((i + 1) % n_lon, i) for i in range(n_lon)])

    n_tiles = total + 1 + (total + 1) % 2
    pairs0 = n_tiles // 2
    pairs1 = (rows + 6) // 2
    tiles = pltpu.VMEM((n_tiles, 8, LANES), F32)
    wide = 2 * LANES
    scratch = (
        [tiles] * 9
        + [pltpu.VMEM((n, 64, wide), BF16) for n in (pairs0, pairs1)]
        + [pltpu.VMEM((n, DEPTH, 2 * HID, wide), BF16) for n in (pairs0, pairs1)]
        + [pltpu.VMEM((n, DEPTH, HID, wide), F32) for n in (pairs0, pairs1)]
        + [pltpu.VMEM((n, DEPTH, HID, wide), F32) for n in (pairs0, pairs1)]
        + [
            pltpu.VMEM((2 * HID, 2 * HID), F32),
            pltpu.VMEM((DEPTH, 2 * HID, 32), F32),
            pltpu.VMEM((HID, wide), F32),
        ]
    )
    final, grad, sums = call(
        functools.partial(steps_kernel, rows),
        [shape(8 * rows, LANES), shape(8 * rows, LANES), shape(HID + 8, LANES)],
        [SMEM] + [VMEM] * 8,
        scratch,
        limit=52 * 1024 * 1024,
        flops=10_000_000_000,
    )(b_head, ext, from_west, from_east, a1, w2t, w2, t1, cols_w)

    rounds = [("lat", 1 << b) for b in range(n_lat.bit_length() - 1)]
    rounds += [("lon", 1 << b) for b in range(n_lon.bit_length() - 1)]
    sizes = {"lat": n_lat, "lon": n_lon}
    for number, (axis, bit) in enumerate(rounds):
        other = lax.ppermute(sums, axis, [(i, i ^ bit) for i in range(sizes[axis])])
        if number < len(rounds) - 1:
            sums = sums + other
    scale = 1.0 / math.sqrt(n_lon * cols * n_lat * rows * DEPTH)
    first_grad, second_grad, head_grad = call(
        functools.partial(finish_kernel, scale),
        [shape(6, HID), shape(HID, HID), shape(1, HID)],
        [VMEM] * 2,
    )(sums, other)
    return (
        final.reshape(tracers.shape),
        grad.reshape(tracers.shape),
        first_grad,
        second_grad,
        head_grad.reshape(HID),
    )


def solution(mesh):
    return jax.shard_map(
        per_device,
        mesh=mesh,
        in_specs=(
            P(None, None, "lat", "lon"),
            P("lat", "lon"),
            P("lat", "lon"),
            P("lon"),
            P(None, None, "lat", "lon"),
            P(),
            P(),
            P(),
            P(),
            P(),
            P(),
        ),
        out_specs=(P(None, None, "lat", "lon"), P(None, None, "lat", "lon"), P(), P(), P()),
        check_vma=False,
    )
```

profile of v0, /device:TPU:0, one launch (start us, length us, event | category | flops | bytes accessed | tf_op | source)
XLA Modules:
  0.0 90.3 jit_solution(4136185495145731054)
XLA Ops:
  0.6 1.5 %shard_map.146 = (f32[48,128]{1,0:T(8,128)}, f32[48,128]{1,0:T(8,128)}) custom-call(f32[128,128]{1,0:T(8,128)} %bitcast.10, f32[128,128]{1,0:T(8,128)} %bitcast.12, s32[16,128]{1,0:T(8,128)} %land.3, s32[16,128]{1,0:T(8,128)} %levels.3), custom_call_target="tpu_custom_call" | custom-call | flops 1000000 | bytes 1000000 | tf_op jit(solution)/shard_map/pallas_call | solution.py:501
  2.1 1.3 %collective-permute-start.16 = (f32[48,128]{1,0:T(8,128)}, f32[48,128]{1,0:T(8,128)S(1)}, u32[]{:S(2)}, u32[]{:S(2)}) collective-permute-start(f32[48,128]{1,0:T(8,128)} %get-tuple-element.30), channel_id=1, source_target_pairs={{1,0},{2,1},{3,2},{5,4},{6,5},{7,6},{9,8},{10,9},{11,10},{13,12},{... | collective-permute-start | bytes 73736 | tf_op jit(solution)/shard_map/ppermute | solution.py:504
  3.4 3.0 %collective-permute-start.17 = (f32[48,128]{1,0:T(8,128)}, f32[48,128]{1,0:T(8,128)S(1)}, u32[]{:S(2)}, u32[]{:S(2)}) collective-permute-start(f32[48,128]{1,0:T(8,128)} %get-tuple-element.31), channel_id=1, source_target_pairs={{0,1},{1,2},{2,3},{4,5},{5,6},{6,7},{8,9},{9,10},{10,11},{12,13},{... | collective-permute-start | bytes 73736 | tf_op jit(solution)/shard_map/ppermute | solution.py:505
  6.5 0.0 copy-start.10
  6.5 0.6 copy-done.10
  7.3 2.6 %conditional.1 = (f32[48,128]{1,0:T(8,128)}, f32[48,128]{1,0:T(8,128)}) conditional(s32[]{:T(128)} %clamp.3, f32[48,128]{1,0:T(8,128)} %get-tuple-element.31, f32[48,128]{1,0:T(8,128)} %get-tuple-element.31, f32[48,128]{1,0:T(8,128)} %get-tuple-element.31, f32[48,128]{1,0:T(8,128)} %get-tuple-element.31, ...), branch_computations={%region_0.1_spmd, %region_1.2_spmd, %region_2.3_spmd, %region_3.4_... | conditional | bytes 196704 | solution.py:521
  7.3 1.3 %collective-permute-start.11 = (f32[48,128]{1,0:T(8,128)}, f32[48,128]{1,0:T(8,128)}, u32[]{:S(2)}, u32[]{:S(2)}) collective-permute-start(f32[48,128]{1,0:T(8,128)} %param.5), channel_id=1, source_target_pairs={{3,19},{7,15},{11,11},{15,7},{19,3},{23,31},{27,27},{31,23}} | collective-permute-start | bytes 73736 | tf_op jit(solution)/shard_map/cond/branch_5_fun/ppermute | solution.py:518
  8.6 1.2 %collective-permute-start.10 = (f32[48,128]{1,0:T(8,128)}, f32[48,128]{1,0:T(8,128)}, u32[]{:S(2)}, u32[]{:S(2)}) collective-permute-start(f32[48,128]{1,0:T(8,128)} %param.5), channel_id=1, source_target_pairs={{3,23},{7,19},{11,15},{15,11},{19,7},{23,3},{27,31},{31,27}} | collective-permute-start | bytes 73736 | tf_op jit(solution)/shard_map/cond/branch_5_fun/ppermute | solution.py:517
  9.8 0.0 collective-permute-done.11
  9.8 0.0 collective-permute-done.10
  9.8 0.0 collective-permute-done.16.from_north
  9.9 0.0 copy-start.8
  9.9 0.0 collective-permute-done.17.from_south
  9.9 0.0 copy-start.9
  9.9 0.6 copy-done.8
  10.5 0.0 copy-done.9
  10.5 1.7 %shard_map.147 = (f32[528,128]{1,0:T(8,128)}, f32[24,128]{1,0:T(8,128)}) custom-call(s32[128]{0:T(128)} %partner.1, f32[48,128]{1,0:T(8,128)} %copy-done.8, f32[48,128]{1,0:T(8,128)} %copy-done.9, f32[48,128]{1,0:T(8,128)} %get-tuple-element.32.fold_near, f32[48,128]{1,0:T(8,128)} %get-tuple-element.33.fold_far, f32[128,128]{1,0:T(8,128)} %bitcast.11, ...), custom_call_target="tpu_custom_call" | custom-call | flops 1000000 | bytes 1000000 | tf_op jit(solution)/shard_map/pallas_call | solution.py:538
  12.2 6.0 %collective-permute-start.19 = (f32[24,128]{1,0:T(8,128)}, f32[24,128]{1,0:T(8,128)S(1)}, u32[]{:S(2)}, u32[]{:S(2)}) collective-permute-start(f32[24,128]{1,0:T(8,128)} %get-tuple-element.35), channel_id=1, source_target_pairs={{4,0},{8,4},{12,8},{16,12},{20,16},{24,20},{28,24},{0,28},{5,1},{9... | collective-permute-start | bytes 36872 | tf_op jit(solution)/shard_map/ppermute | solution.py:554
  18.2 0.0 collective-permute-start.18
  18.9 1.8 %shard_map.148 = (bf16[512,64]{1,0:T(8,128)(2,1)}, bf16[256,256]{1,0:T(8,128)(2,1)}, bf16[256,256]{1,0:T(8,128)(2,1)}, bf16[128,256]{1,0:T(8,128)(2,1)}, f32[256,256]{1,0:T(8,128)}) custom-call(f32[6,128]{1,0:T(8,128)} %w1.1, f32[1,128]{1,0:T(1,128)} %bitcast.18, f32[128,128]{1,0:T(8,128)} %w2.1, f32[1,128]{1,0:T(1,128)} %bitcast.19, f32[1,128]{1,0:T(1,128)} %bitcast.20), custom_call_target="tpu_custom_call" | custom-call | flops 1000000 | bytes 1000000 | tf_op jit(solution)/shard_map/pallas_call | solution.py:525
  20.7 0.0 collective-permute-done.19.east_in
  20.7 4.1 %collective-permute-done.18.west_in = f32[24,128]{1,0:T(8,128)S(1)} collective-permute-done((f32[24,128]{1,0:T(8,128)}, f32[24,128]{1,0:T(8,128)S(1)}, u32[]{:S(2)}, u32[]{:S(2)}) %collective-permute-start.18) | collective-permute-done | bytes 12320 | tf_op jit(solution)/shard_map/ppermute | solution.py:553
  24.8 0.0 copy-start
  24.8 1.0 %copy-done = f32[528,128]{1,0:T(8,128)S(1)} copy-done((f32[528,128]{1,0:T(8,128)S(1)}, f32[528,128]{1,0:T(8,128)}, u32[]{:S(2)}) %copy-start) | copy-done | bytes 270360
  25.8 0.0 copy-start.1
  25.8 0.9 %copy-done.1 = f32[256,256]{1,0:T(8,128)S(1)} copy-done((f32[256,256]{1,0:T(8,128)S(1)}, f32[256,256]{1,0:T(8,128)}, u32[]{:S(2)}) %copy-start.1) | copy-done | bytes 262168
  26.7 0.0 copy-start.2
  26.7 0.9 copy-done.2
  27.6 0.0 copy-start.3
  27.7 0.9 copy-done.3
  28.6 0.0 copy-start.4
  28.6 0.9 copy-done.4
  29.5 0.0 copy-start.5
  29.5 0.8 copy-done.5
  30.3 36.0 %shard_map.149 = (f32[128,128]{1,0:T(8,128)}, f32[128,128]{1,0:T(8,128)}, f32[136,128]{1,0:T(8,128)S(1)}) custom-call(f32[1]{0:T(128)S(6)} %copy.32.head_bias, f32[528,128]{1,0:T(8,128)S(1)} %copy-done, f32[24,128]{1,0:T(8,128)S(1)} %collective-permute-done.18.west_in, f32[24,128]{1,0:T(8,128)S(1)} %collective-permute-done.19.east_in, ...), custom_call_target="tpu_custom_call" | custom-call | flops 10000000000 | bytes 1000000 | tf_op jit(solution)/shard_map/pallas_call | solution.py:573
  66.3 0.0 collective-permute-start.20
  66.3 1.3 %collective-permute-done.20 = f32[136,128]{1,0:T(8,128)S(1)} collective-permute-done((f32[136,128]{1,0:T(8,128)S(1)}, f32[136,128]{1,0:T(8,128)S(1)}, u32[]{:S(2)}, u32[]{:S(2)}) %collective-permute-start.20) | collective-permute-done | bytes 69664 | tf_op jit(solution)/shard_map/ppermute | solution.py:586
  67.6 3.6 %collective-permute-start.21 = (f32[136,128]{1,0:T(8,128)S(1)}, f32[136,128]{1,0:T(8,128)S(1)}, u32[]{:S(2)}, u32[]{:S(2)}) collective-permute-start(f32[136,128]{1,0:T(8,128)S(1)} %add.17), channel_id=1, source_target_pairs={{0,2},{1,3},{2,0},{3,1},{4,6},{5,7},{6,4},{7,5},{8,10},{9,11},{10,... | collective-permute-start | bytes 208904 | tf_op jit(solution)/shard_map/ppermute | solution.py:586
  71.2 2.7 %collective-permute-done.21 = f32[136,128]{1,0:T(8,128)S(1)} collective-permute-done((f32[136,128]{1,0:T(8,128)S(1)}, f32[136,128]{1,0:T(8,128)S(1)}, u32[]{:S(2)}, u32[]{:S(2)}) %collective-permute-start.21) | collective-permute-done | bytes 69664 | tf_op jit(solution)/shard_map/ppermute | solution.py:586
  73.9 0.1 collective-permute-start.22
  74.0 4.3 %collective-permute-done.22 = f32[136,128]{1,0:T(8,128)S(1)} collective-permute-done((f32[136,128]{1,0:T(8,128)S(1)}, f32[136,128]{1,0:T(8,128)S(1)}, u32[]{:S(2)}, u32[]{:S(2)}) %collective-permute-start.22) | collective-permute-done | bytes 69664 | tf_op jit(solution)/shard_map/ppermute | solution.py:586
  78.3 0.1 collective-permute-start.23
  78.4 4.3 %collective-permute-done.23 = f32[136,128]{1,0:T(8,128)S(1)} collective-permute-done((f32[136,128]{1,0:T(8,128)S(1)}, f32[136,128]{1,0:T(8,128)S(1)}, u32[]{:S(2)}, u32[]{:S(2)}) %collective-permute-start.23) | collective-permute-done | bytes 69664 | tf_op jit(solution)/shard_map/ppermute | solution.py:586
  82.7 0.0 copy-start.6
  82.7 0.2 collective-permute-start.24
  82.9 5.2 %collective-permute-done.24.other = f32[136,128]{1,0:T(8,128)S(1)} collective-permute-done((f32[136,128]{1,0:T(8,128)S(1)}, f32[136,128]{1,0:T(8,128)S(1)}, u32[]{:S(2)}, u32[]{:S(2)}) %collective-permute-start.24) | collective-permute-done | bytes 69664 | tf_op jit(solution)/shard_map/ppermute | solution.py:586
  88.2 0.0 copy-done.6
  88.2 0.0 copy-start.7
  88.2 0.6 copy-done.7
  88.8 1.6 %shard_map.150 = (f32[6,128]{1,0:T(8,128)}, f32[128,128]{1,0:T(8,128)}, f32[1,128]{1,0:T(1,128)}) custom-call(f32[136,128]{1,0:T(8,128)} %copy-done.6, f32[136,128]{1,0:T(8,128)} %copy-done.7), custom_call_target="tpu_custom_call" | custom-call | flops 1000000 | bytes 1000000 | tf_op jit(solution)/shard_map/pallas_call | solution.py:590
  (4 shorter events, 0.0 us)
Async XLA Ops:
  2.1 7.7 %collective-permute-start.16 = (f32[48,128]{1,0:T(8,128)}, f32[48,128]{1,0:T(8,128)S(1)}, u32[]{:S(2)}, u32[]{:S(2)}) collective-permute-start(f32[48,128]{1,0:T(8,128)} %get-tuple-element.30), channel_id=1, source_target_pairs={{1,0},{2,1},{3,2},{5,4},{6,5},{7,6},{9,8},{10,9},{11,10},{13,12},{... | collective-permute-start | bytes 73736 | tf_op jit(solution)/shard_map/ppermute | solution.py:504
  3.4 6.4 %collective-permute-start.17 = (f32[48,128]{1,0:T(8,128)}, f32[48,128]{1,0:T(8,128)S(1)}, u32[]{:S(2)}, u32[]{:S(2)}) collective-permute-start(f32[48,128]{1,0:T(8,128)} %get-tuple-element.31), channel_id=1, source_target_pairs={{0,1},{1,2},{2,3},{4,5},{5,6},{6,7},{8,9},{9,10},{10,11},{12,13},{... | collective-permute-start | bytes 73736 | tf_op jit(solution)/shard_map/ppermute | solution.py:505
  6.5 0.7 copy-start.10
  7.3 2.5 %collective-permute-start.11 = (f32[48,128]{1,0:T(8,128)}, f32[48,128]{1,0:T(8,128)}, u32[]{:S(2)}, u32[]{:S(2)}) collective-permute-start(f32[48,128]{1,0:T(8,128)} %param.5), channel_id=1, source_target_pairs={{3,19},{7,15},{11,11},{15,7},{19,3},{23,31},{27,27},{31,23}} | collective-permute-start | bytes 73736 | tf_op jit(solution)/shard_map/cond/branch_5_fun/ppermute | solution.py:518
  8.6 1.3 %collective-permute-start.10 = (f32[48,128]{1,0:T(8,128)}, f32[48,128]{1,0:T(8,128)}, u32[]{:S(2)}, u32[]{:S(2)}) collective-permute-start(f32[48,128]{1,0:T(8,128)} %param.5), channel_id=1, source_target_pairs={{3,23},{7,19},{11,15},{15,11},{19,7},{23,3},{27,31},{31,27}} | collective-permute-start | bytes 73736 | tf_op jit(solution)/shard_map/cond/branch_5_fun/ppermute | solution.py:517
  9.9 0.6 copy-start.8
  9.9 0.6 copy-start.9
  12.2 8.5 %collective-permute-start.19 = (f32[24,128]{1,0:T(8,128)}, f32[24,128]{1,0:T(8,128)S(1)}, u32[]{:S(2)}, u32[]{:S(2)}) collective-permute-start(f32[24,128]{1,0:T(8,128)} %get-tuple-element.35), channel_id=1, source_target_pairs={{4,0},{8,4},{12,8},{16,12},{20,16},{24,20},{28,24},{0,28},{5,1},{9... | collective-permute-start | bytes 36872 | tf_op jit(solution)/shard_map/ppermute | solution.py:554
  18.2 6.6 %collective-permute-start.18 = (f32[24,128]{1,0:T(8,128)}, f32[24,128]{1,0:T(8,128)S(1)}, u32[]{:S(2)}, u32[]{:S(2)}) collective-permute-start(f32[24,128]{1,0:T(8,128)} %get-tuple-element.35), channel_id=1, source_target_pairs={{0,4},{4,8},{8,12},{12,16},{16,20},{20,24},{24,28},{28,0},{1,5},{5... | collective-permute-start | bytes 36872 | tf_op jit(solution)/shard_map/ppermute | solution.py:553
  24.8 1.0 %copy-start = (f32[528,128]{1,0:T(8,128)S(1)}, f32[528,128]{1,0:T(8,128)}, u32[]{:S(2)}) copy-start(f32[528,128]{1,0:T(8,128)} %get-tuple-element.34.ext) | copy-start | bytes 811012
  25.8 0.9 %copy-start.1 = (f32[256,256]{1,0:T(8,128)S(1)}, f32[256,256]{1,0:T(8,128)}, u32[]{:S(2)}) copy-start(f32[256,256]{1,0:T(8,128)} %get-tuple-element.40.cols) | copy-start | bytes 786436
  26.7 0.9 %copy-start.2 = (bf16[512,64]{1,0:T(8,128)(2,1)S(1)}, bf16[512,64]{1,0:T(8,128)(2,1)}, u32[]{:S(2)}) copy-start(bf16[512,64]{1,0:T(8,128)(2,1)} %get-tuple-element.36.a1) | copy-start | bytes 196612
  27.6 0.9 %copy-start.3 = (bf16[256,256]{1,0:T(8,128)(2,1)S(1)}, bf16[256,256]{1,0:T(8,128)(2,1)}, u32[]{:S(2)}) copy-start(bf16[256,256]{1,0:T(8,128)(2,1)} %get-tuple-element.37.w2t) | copy-start | bytes 393220
  28.6 0.9 %copy-start.4 = (bf16[256,256]{1,0:T(8,128)(2,1)S(1)}, bf16[256,256]{1,0:T(8,128)(2,1)}, u32[]{:S(2)}) copy-start(bf16[256,256]{1,0:T(8,128)(2,1)} %get-tuple-element.38.w2) | copy-start | bytes 393220
  29.5 0.8 copy-start.5
  66.3 1.3 %collective-permute-start.20 = (f32[136,128]{1,0:T(8,128)S(1)}, f32[136,128]{1,0:T(8,128)S(1)}, u32[]{:S(2)}, u32[]{:S(2)}) collective-permute-start(f32[136,128]{1,0:T(8,128)S(1)} %get-tuple-element.43), channel_id=1, source_target_pairs={{0,1},{1,0},{2,3},{3,2},{4,5},{5,4},{6,7},{7,6},{8,9},{9,8},{10,11... | collective-permute-start | bytes 208904 | tf_op jit(solution)/shard_map/ppermute | solution.py:586
  67.6 6.3 %collective-permute-start.21 = (f32[136,128]{1,0:T(8,128)S(1)}, f32[136,128]{1,0:T(8,128)S(1)}, u32[]{:S(2)}, u32[]{:S(2)}) collective-permute-start(f32[136,128]{1,0:T(8,128)S(1)} %add.17), channel_id=1, source_target_pairs={{0,2},{1,3},{2,0},{3,1},{4,6},{5,7},{6,4},{7,5},{8,10},{9,11},{10,... | collective-permute-start | bytes 208904 | tf_op jit(solution)/shard_map/ppermute | solution.py:586
  73.9 4.4 %collective-permute-start.22 = (f32[136,128]{1,0:T(8,128)S(1)}, f32[136,128]{1,0:T(8,128)S(1)}, u32[]{:S(2)}, u32[]{:S(2)}) collective-permute-start(f32[136,128]{1,0:T(8,128)S(1)} %add.18), channel_id=1, source_target_pairs={{0,4},{4,0},{8,12},{12,8},{16,20},{20,16},{24,28},{28,24},{1,5},{5... | collective-permute-start | bytes 208904 | tf_op jit(solution)/shard_map/ppermute | solution.py:586
  78.3 4.4 %collective-permute-start.23 = (f32[136,128]{1,0:T(8,128)S(1)}, f32[136,128]{1,0:T(8,128)S(1)}, u32[]{:S(2)}, u32[]{:S(2)}) collective-permute-start(f32[136,128]{1,0:T(8,128)S(1)} %add.19), channel_id=1, source_target_pairs={{0,8},{4,12},{8,0},{12,4},{16,24},{20,28},{24,16},{28,20},{1,9},{5... | collective-permute-start | bytes 208904 | tf_op jit(solution)/shard_map/ppermute | solution.py:586
  82.7 5.5 %copy-start.6 = (f32[136,128]{1,0:T(8,128)}, f32[136,128]{1,0:T(8,128)S(1)}, u32[]{:S(2)}) copy-start(f32[136,128]{1,0:T(8,128)S(1)} %add.20.mine) | copy-start | bytes 208900
  82.7 5.5 %collective-permute-start.24 = (f32[136,128]{1,0:T(8,128)S(1)}, f32[136,128]{1,0:T(8,128)S(1)}, u32[]{:S(2)}, u32[]{:S(2)}) collective-permute-start(f32[136,128]{1,0:T(8,128)S(1)} %add.20.mine), channel_id=1, source_target_pairs={{0,16},{4,20},{8,24},{12,28},{16,0},{20,4},{24,8},{28,12},{1,17},{... | collective-permute-start | bytes 208904 | tf_op jit(solution)/shard_map/ppermute | solution.py:586
  88.2 0.6 copy-start.7
where the time goes:
time: 90.9 us; the launch traced here: 90.3 us
  Pallas kernels  42.7 us (47%)
  waiting for transfers between devices  21.9 us (24%)
  starting transfers between devices  16.8 us (18%)
  local copies, waits for them, and re-layouts  7.33 us (8%)
  between operations  1.56 us (2%)
    pallas_call x1, Pallas kernels, per_device(): call(functools.partial(steps_kernel, rows), [shape(8 * rows, LANES), shap...  36 us
    ppermute x5, waiting for transfers between devices, per_device(): other = lax.ppermute(sums, axis, [(i, i ^ bit) for i in range(sizes[axis])])  17.8 us
    unnamed x22, local copies, waits for them, and re-layouts  7.33 us
    ppermute x1, starting transfers between devices, per_device(): lax.ppermute(packed, 'lon', [((i + 1) % n_lon, i) for i in range(n_lon)])  6 us
    ppermute x1, waiting for transfers between devices, per_device(): lax.ppermute(packed, 'lon', [(i, (i + 1) % n_lon) for i in range(n_lon)])  4.1 us
    ppermute x5, starting transfers between devices, per_device(): other = lax.ppermute(sums, axis, [(i, i ^ bit) for i in range(sizes[axis])])  3.96 us
    ppermute x1, starting transfers between devices, per_device(): lax.ppermute(north, 'lat', [(i, i + 1) for i in range(n_lat - 1)])  3.03 us
    pallas_call x1, Pallas kernels, per_device(): call(weights_kernel, [shape(DEPTH * HID, 64, dtype=BF16), shape(2 * HID,...  1.84 us
  transfers between devices with their start and end apart: 11, of which 6 were waited for; matrix products, arithmetic and copies ran while one was open for 0% of the time, Pallas kernels for 2%

commit v1 on v0

v1 whole, which is shorter than its diff:
```python
import functools
import math

import jax
import jax.numpy as jnp
from jax import lax
from jax.experimental import pallas as pl
from jax.experimental.pallas import tpu as pltpu
from jax.sharding import PartitionSpec as P

KMAX = 0.24
DEPTH = 4
HID = 128
LANES = 128
HALO = 3
SLOT = 2 * HALO
F32 = jnp.float32
BF16 = jnp.bfloat16


def split(x):
    high = x.astype(BF16)
    low = (x - high.astype(F32)).astype(BF16)
    return high, low


def iota(shape, dim):
    return lax.broadcasted_iota(jnp.int32, shape, dim)


def prepare_kernel(
    rows,
    cols,
    tracer_hbm,
    cot_hbm,
    land_hbm,
    levels_hbm,
    partner_hbm,
    w1_hbm,
    b1_hbm,
    w2_hbm,
    b2_hbm,
    wh_hbm,
    bh_hbm,
    south_first,
    north,
    south_last,
    turn_out,
    offset_out,
    own_out,
    a1_out,
    w2t_out,
    w2_out,
    col_out,
    tracer,
    cot,
    land,
    levels,
    partner,
    w1,
    b1,
    w2,
    b2,
    wh,
    bh,
    sems,
):
    copies = [
        pltpu.make_async_copy(source, target, sems.at[n])
        for n, (source, target) in enumerate(
            (
                (partner_hbm, partner),
                (tracer_hbm, tracer),
                (cot_hbm, cot),
                (land_hbm, land),
                (levels_hbm, levels),
                (w1_hbm, w1),
                (b1_hbm, b1),
                (w2_hbm, w2),
                (b2_hbm, b2),
                (wh_hbm, wh),
                (bh_hbm, bh),
            )
        )
    ]
    for copy in copies:
        copy.start()
    for copy in copies:
        copy.wait()
    here = partner[0]
    n_lon = lax.axis_size("lon")
    turn_out[0] = lax.rem(lax.div(here, cols) + lax.axis_index("lon"), n_lon)
    offset_out[...] = jnp.full((8, LANES), lax.rem(here, cols), jnp.int32)

    at_top = lax.axis_index("lat") == lax.axis_size("lat") - 1
    depth = (land[...] * levels[...]).astype(F32)
    for r in range(rows):
        own_out[24 * r : 24 * r + 8, :] = tracer[pl.ds(r, 8, stride=rows), :]
        own_out[24 * r + 8 : 24 * r + 16, :] = cot[pl.ds(r, 8, stride=rows), :]
        own_out[24 * r + 16 : 24 * r + 24, :] = jnp.broadcast_to(depth[r : r + 1], (8, LANES))

    def edge(first, skip):
        parts = [tracer[pl.ds(first + j, 8, stride=rows), :] for j in range(HALO)]
        parts += [cot[pl.ds(first + skip + j, 8, stride=rows), :] for j in range(2)]
        parts += [depth[first : first + HALO], jnp.zeros((8 - HALO, LANES), F32)]
        return jnp.concatenate(parts, 0)

    low, high = edge(0, 0), edge(rows - HALO, 1)
    south_first[...] = jnp.where(at_top, high, low)
    north[...] = high
    south_last[...] = jnp.where(at_top, low, high)
    prepare_weights(w1, b1, w2, b2, wh, bh, a1_out, w2t_out, w2_out, col_out)


def prepare_weights(w1, b1, w2, b2, wh, bh, a1_out, w2t_out, w2_out, col_out):
    first = w1[...]
    bias_high, bias_low = split(b1[...])
    row = iota((16, LANES), 0)
    pad_row = iota((16, LANES), 0)
    for k in range(DEPTH):
        block = jnp.zeros((16, LANES), F32)
        for t in range(2):
            block = jnp.where(row == t * 4 + k, first[t : t + 1], block)
            if k >= 1:
                block = jnp.where(row == 8 + t * 4 + k - 1, -first[2 + t : 3 + t], block)
            block = jnp.where(row == 8 + t * 4 + k, first[4 + t : 5 + t], block)
        high, low = split(block)
        high32, low32 = high.astype(F32), low.astype(F32)
        tail = jnp.where(
            pad_row == 0,
            bias_high.astype(F32),
            jnp.where(pad_row == 1, bias_low.astype(F32), 0.0),
        )
        tall = jnp.concatenate([high32, high32, low32, tail, jnp.zeros((64, LANES), F32)], 0)
        a1_out[k * HID : (k + 1) * HID, :] = jnp.transpose(tall)[:, :64].astype(BF16)
    second = w2[...]
    for out, matrix in ((w2_out, second), (w2t_out, jnp.transpose(second))):
        high, low = split(matrix)
        out[0:HID, :] = jnp.concatenate([high, high], 1)
        out[HID : 2 * HID, :] = jnp.concatenate([low, low], 1)
    vectors = [b2[...], wh[...]] + [first[f : f + 1] for f in range(6)]
    for n, vector in enumerate(vectors):
        column = jnp.transpose(jnp.broadcast_to(vector, (HID, LANES)))
        col_out[n * HID : (n + 1) * HID, :] = column
    col_out[8 * HID : 8 * HID + 8, :] = jnp.full((8, LANES), bh[0], F32)


def assemble_kernel(rows, offset_in, first, second, third, own, halo, packed):
    lane = iota((8, LANES), 1)
    lat, n_lat = lax.axis_index("lat"), lax.axis_size("lat")
    at_top = lat == n_lat - 1
    below_top = lat == n_lat - 2
    at_bottom = lat == 0
    offset = offset_in[...]
    source = jnp.bitwise_and(offset - lane, LANES - 1)

    def mirrored(place):
        both = jnp.where(
            lane <= offset, first[place : place + 8, :], second[place : place + 8, :]
        )
        return jnp.take_along_axis(both, source, axis=1)

    zero = jnp.zeros((8, LANES), F32)

    def from_north(place):
        return jnp.where(below_top, third[place : place + 8, :], first[place : place + 8, :])

    def from_south(place):
        near = jnp.where(at_top, third[place : place + 8, :], second[place : place + 8, :])
        return jnp.where(at_bottom, 0.0, near)

    def north(plain, folded):
        return jnp.where(at_top, mirrored(folded), from_north(plain))

    def spread(tile, j):
        return jnp.broadcast_to(tile[j : j + 1], (8, LANES))

    depth_south = from_south(40)
    depth_north = from_north(40)
    depth_fold = mirrored(40)
    total = rows + 2 * HALO
    tiles = []
    for i in range(total):
        r = i - HALO
        if r < 0:
            tile_c = from_south(8 * i)
            tile_l = from_south(24 + 8 * (i - 1)) if i >= 1 else zero
            tile_n = spread(depth_south, i)
        elif r < rows:
            tile_c = own[24 * r : 24 * r + 8, :]
            tile_l = own[24 * r + 8 : 24 * r + 16, :]
            tile_n = own[24 * r + 16 : 24 * r + 24, :]
        else:
            j = r - rows
            tile_c = north(8 * j, 8 * (2 - j))
            tile_l = north(24 + 8 * j, 24 + 8 * (1 - j)) if j < 2 else zero
            tile_n = jnp.where(at_top, spread(depth_fold, 2 - j), spread(depth_north, j))
        tiles.append((tile_c, tile_l, tile_n))
        place = 24 * (i if r < 0 else i - rows)
        if not 0 <= r < rows:
            for part, tile in enumerate(tiles[-1]):
                halo[place + 8 * part : place + 8 * part + 8, :] = tile
    for part in range(3):
        acc = zero
        for slot in range(rows + 4):
            moved = pltpu.roll(tiles[slot + 1][part], SLOT * slot + HALO, 1)
            inside = (lane >= SLOT * slot) & (lane < SLOT * slot + SLOT)
            acc = jnp.where(inside, moved, acc)
        packed[8 * part : 8 * part + 8, :] = acc


def steps_kernel(
    rows,
    own_rows,
    halo_rows,
    west_in,
    east_in,
    a1,
    w2t,
    w2,
    cols,
    out_tracer,
    out_grad,
    out_keep,
    out_give,
    c_tiles0,
    c_tiles1,
    wv_tiles,
    wet_tiles,
    kappa_tiles,
    slope0,
    slope1,
    d3_tiles,
    bar_tiles,
    x0,
    x1,
    h1b0,
    h1b1,
    h1f0,
    h1f1,
    h2f0,
    h2f1,
    acc_w2,
    acc_a1,
    acc_head,
):
    total = rows + 2 * HALO
    lane = iota((8, LANES), 1)
    level = jnp.bitwise_and(iota((8, LANES), 0), DEPTH - 1)
    level_wide = jnp.bitwise_and(iota((8, 2 * LANES), 0), DEPTH - 1)
    zero = jnp.zeros((8, LANES), F32)
    side_tile = rows
    tile_of = {i: i - HALO for i in range(HALO, rows + HALO)}
    place = rows + 1
    for ring in (1, 2, 3):
        tile_of[HALO - ring] = place
        tile_of[rows + HALO - 1 + ring] = place + 1
        place += 2
    n_tiles = place + (place % 2)
    slots = range(1, rows + 5)

    def east(main, side):
        return (
            pltpu.roll(jnp.where(lane == 0, side, main), LANES - 1, 1),
            pltpu.roll(jnp.where(lane == 0, main, side), LANES - 1, 1),
        )

    def from_west(main, side):
        return (
            pltpu.roll(jnp.where(lane == LANES - 1, side, main), 1, 1),
            pltpu.roll(jnp.where(lane == LANES - 1, main, side), 1, 1),
        )

    def from_west_main(main, side):
        return pltpu.roll(jnp.where(lane == LANES - 1, side, main), 1, 1)

    def unpack(tile, i):
        return pltpu.roll(tile, LANES - (SLOT * (i - 1) + HALO), 1)

    def pack(tiles):
        acc = zero
        for i, tile in tiles.items():
            slot = i - 1
            moved = pltpu.roll(tile, SLOT * slot + HALO, 1)
            inside = (lane >= SLOT * slot) & (lane < SLOT * slot + SLOT)
            acc = jnp.where(inside, moved, acc)
        return acc

    def column(n):
        part = cols[n * HID : (n + 1) * HID, :]
        return jnp.concatenate([part, part], 1)

    head_bias = cols[8 * HID : 8 * HID + 1, :][:, 0:1]

    def both(x):
        return x + pltpu.roll(x, 4, 0)

    third = lax.rem(lane, SLOT)
    from_left = third < HALO
    side_c_packed = jnp.where(from_left, west_in[0:8, :], east_in[0:8, :])
    side_l_packed = jnp.where(from_left, west_in[8:16, :], east_in[8:16, :])
    side_n_packed = jnp.where(from_left, west_in[16:24, :], east_in[16:24, :])
    side_lanes = (lane < HALO) | (lane >= LANES - HALO)

    def wet_of(depth):
        return jnp.where(depth > level.astype(F32), 1.0, 0.0)

    def vertical_of(depth):
        inside = (depth > (level + 1).astype(F32)) & (level < DEPTH - 1)
        return jnp.where(inside, 1.0, 0.0)

    def tile_at(i, part):
        if HALO <= i < rows + HALO:
            place = 24 * (i - HALO) + 8 * part
            return own_rows[place : place + 8, :]
        place = 24 * (i if i < HALO else i - rows) + 8 * part
        return halo_rows[place : place + 8, :]

    c0, wet = {}, {}
    for i in range(total):
        depth = tile_at(i, 2)
        main_c = tile_at(i, 0)
        main_w = wet_of(depth)
        if i in slots:
            side_c = unpack(side_c_packed, i)
            side_w = jnp.where(side_lanes, wet_of(unpack(side_n_packed, i)), 0.0)
        else:
            side_c, side_w = zero, zero
        c0[i] = (main_c, side_c)
        wet[i] = (main_w, side_w)
        c_tiles0[tile_of[i]] = main_c
        wet_tiles[tile_of[i]] = main_w
        wv_tiles[tile_of[i]] = vertical_of(depth)
    c_tiles0[side_tile] = side_c_packed
    wet_tiles[side_tile] = wet_of(side_n_packed)
    wv_tiles[side_tile] = vertical_of(side_n_packed)
    for tile in range(place, n_tiles):
        c_tiles0[tile] = zero
        wet_tiles[tile] = zero
        wv_tiles[tile] = zero

    def closure(start, steps, group, save, c_tiles, slope, xs, h1b, h1f, h2f):
        def body(step, carry):
            first_pair = start + step * group
            items = [(first_pair + g, k) for g in range(group) for k in range(DEPTH)]
            inputs = []
            for g in range(group):
                p = first_pair + g
                pieces = []
                for a in range(2):
                    c = c_tiles[2 * p + a]
                    v = (pltpu.roll(c, 7, 0) - c) * wv_tiles[2 * p + a]
                    pieces.append(jnp.concatenate([c, v], 0))
                high, low = split(jnp.concatenate(pieces, 1))
                x = jnp.concatenate([high, low, high, jnp.ones((16, 2 * LANES), BF16)], 0)
                if save:
                    xs[p] = x
                inputs.append(jnp.dot(a1[...], x, preferred_element_type=F32))
            outs = [jnp.zeros((8, 2 * LANES), F32)] * group
            pairs = {}
            for j in range(len(items) + 1):
                if j < len(items):
                    p, k = items[j]
                    h1 = jnp.tanh(inputs[j // DEPTH][k * HID : (k + 1) * HID])
                    pairs[j] = jnp.concatenate(split(h1), 0)
                    if save:
                        h1f[p, k] = h1
                        h1b[p, k] = pairs[j]
                if j >= 1:
                    p, k = items[j - 1]
                    z = jnp.dot(w2t[...], pairs.pop(j - 1), preferred_element_type=F32)
                    h2 = jnp.tanh(z[:HID] + z[HID:] + column(0))
                    if save:
                        h2f[p, k] = h2
                    head = jnp.sum(h2 * column(1), 0, keepdims=True)
                    g = (j - 1) // DEPTH
                    outs[g] = jnp.where(level_wide == k, head, outs[g])
            for g in range(group):
                sig = jax.nn.sigmoid(outs[g] + head_bias)
                for a in range(2):
                    tile = 2 * (first_pair + g) + a
                    part = sig[:, a * LANES : (a + 1) * LANES]
                    kappa = KMAX * part * wet_tiles[tile]
                    kappa_tiles[tile] = kappa
                    slope[tile] = kappa * (1.0 - part)
            return carry

        lax.fori_loop(0, steps, body, 0)

    def edge_masks(i):
        east_w = east(*wet[i])
        return tuple(0.5 * a * b for a, b in zip(wet[i], east_w))

    def north_mask(i):
        return tuple(0.5 * a * b for a, b in zip(wet[i], wet[i + 1]))

    def kappas(lo, hi):
        packed = kappa_tiles[side_tile]
        out = {}
        for i in range(lo, hi + 1):
            side = unpack(packed, i) if i in slots else zero
            out[i] = (kappa_tiles[tile_of[i]], side)
        return out

    def coefficients(kappa, lo, hi):
        ce, cn = {}, {}
        for i in range(lo, hi + 1):
            ke = east(*kappa[i])
            ce[i] = tuple(m * (a + b) for m, a, b in zip(edge_masks(i), kappa[i], ke))
        for i in range(lo - 1, hi + 1):
            cn[i] = tuple(
                m * (a + b) for m, a, b in zip(north_mask(i), kappa[i], kappa[i + 1])
            )
        return ce, cn

    def diffs(field, lo, hi):
        de, dn = {}, {}
        for i in range(lo, hi + 1):
            fe = east(*field[i])
            de[i] = tuple(b - a for a, b in zip(field[i], fe))
        for i in range(lo - 1, hi + 1):
            dn[i] = tuple(b - a for a, b in zip(field[i], field[i + 1]))
        return de, dn

    def diffuse(field, ce, cn, de, dn, lo, hi):
        out = {}
        flux_n = {i: tuple(c * d for c, d in zip(cn[i], dn[i])) for i in range(lo - 1, hi + 1)}
        for i in range(lo, hi + 1):
            fe = tuple(c * d for c, d in zip(ce[i], de[i]))
            fw = from_west(*fe)
            out[i] = tuple(
                f + ((a - b) + (c - d))
                for f, a, b, c, d in zip(field[i], fe, fw, flux_n[i], flux_n[i - 1])
            )
        return out

    def kappa_bars(de, dn, le, ln, lo, hi):
        out = {}
        gn = {}
        for i in range(lo - 1, hi + 1):
            gn[i] = tuple(-m * a * b for m, a, b in zip(north_mask(i), dn[i], ln[i]))
        for i in range(lo, hi + 1):
            ge = tuple(-m * a * b for m, a, b in zip(edge_masks(i), de[i], le[i]))
            gw = from_west(*ge)
            out[i] = tuple(
                both((a + b) + (c + d)) for a, b, c, d in zip(ge, gw, gn[i], gn[i - 1])
            )
        return out

    def outer(left, right):
        return lax.dot_general(
            left, right, (((1,), (1,)), ((), ())), preferred_element_type=F32
        )

    sublane_wide = iota((8, 2 * LANES), 0)

    def groups(x):
        return jnp.sum(x.reshape(HID // 8, 8, 2 * LANES), 0)

    def put_row(bars, n, row, part):
        value = jnp.where(sublane_wide == row, jnp.sum(part, 0, keepdims=True), 0.0)
        bars = list(bars)
        bars[n] = plus(bars[n], value)
        return bars

    def plus(left, right):
        return right if left is None else left + right

    def closure_back(start, steps, group, with_sums, slope, xs, h1b, h1f, h2f):
        def body(step, carry):
            first_pair = start + step * group
            items = [(first_pair + g, k) for g in range(group) for k in range(DEPTH)]
            d3 = [
                jnp.concatenate(
                    [
                        d3_tiles[2 * (first_pair + g) + a] * slope[2 * (first_pair + g) + a]
                        for a in range(2)
                    ],
                    1,
                )
                for g in range(group)
            ]
            bars = [[None] * 6 for g in range(group)]
            sum_w2, sum_head, sum_a1 = None, None, None
            seconds, firsts = {}, {}
            for j in range(len(items) + 2):
                if j < len(items):
                    p, k = items[j]
                    h2 = h2f[p, k]
                    row = d3[j // DEPTH][k : k + 1]
                    d2 = (column(1) * row) * (1.0 - h2 * h2)
                    seconds[j] = jnp.concatenate(split(d2), 0)
                    if with_sums:
                        sum_head = plus(sum_head, h2 * row)
                if 1 <= j <= len(items):
                    p, k = items[j - 1]
                    d2b = seconds.pop(j - 1)
                    e = jnp.dot(w2[...], d2b, preferred_element_type=F32)
                    h1 = h1f[p, k]
                    d1 = (e[:HID] + e[HID:]) * (1.0 - h1 * h1)
                    firsts[j - 1] = d1
                    if with_sums:
                        sum_w2 = plus(sum_w2, outer(h1b[p, k], d2b))
                if j >= 2:
                    p, k = items[j - 2]
                    g = (j - 2) // DEPTH
                    d1 = firsts.pop(j - 2)
                    if with_sums:
                        seconds[g, k] = jnp.concatenate(split(d1), 0)
                        if k == DEPTH - 1:
                            d1b = jnp.concatenate([seconds.pop((g, n)) for n in range(DEPTH)], 0)
                            sum_a1 = plus(sum_a1, outer(d1b, xs[p, 0:32, :]))
                    parts = [groups(d1 * column(2 + f)) for f in range(6)]
                    for t in range(2):
                        bars[g] = put_row(bars[g], t, t * DEPTH + k, parts[t])
                        if k >= 1:
                            below = bars[g][2 + t]
                            bars[g] = put_row(
                                bars[g], 4 + t, t * DEPTH + k - 1, below - parts[2 + t]
                            )
                        bars[g][2 + t] = parts[4 + t]
            if with_sums:
                acc_w2[...] += sum_w2
                acc_head[...] += sum_head
                acc_a1[...] += sum_a1
            for g in range(group):
                cells = plus(bars[g][0], bars[g][1])
                vertical = plus(bars[g][4], bars[g][5])
                for a in range(2):
                    tile = 2 * (first_pair + g) + a
                    lanes = slice(a * LANES, (a + 1) * LANES)
                    v = vertical[:, lanes] * wv_tiles[tile]
                    bar_tiles[tile] = cells[:, lanes] - v + pltpu.roll(v, 1, 0)
            return carry

        lax.fori_loop(0, steps, body, 0)

    low, high = HALO, rows + HALO - 1
    step0 = (c_tiles0, slope0, x0, h1b0, h1f0, h2f0)
    own = rows // 2
    closure(0, own // 4, 4, True, *step0)
    closure(own, (n_tiles // 2 - own) // 2, 2, False, *step0)
    kappa0 = kappas(0, total - 1)
    ce0, cn0 = coefficients(kappa0, low - 2, high + 2)
    de0, dn0 = diffs(c0, low - 2, high + 2)
    c1 = diffuse(c0, ce0, cn0, de0, dn0, low - 2, high + 2)
    for i in range(low - 2, high + 3):
        c_tiles1[tile_of[i]] = c1[i][0]
    c_tiles1[side_tile] = pack({i: c1[i][1] for i in range(low - 2, high + 3)})
    tiles1 = rows + 5
    for tile in range(tiles1, n_tiles):
        c_tiles1[tile] = zero
    step1 = (c_tiles1, slope1, x1, h1b1, h1f1, h2f1)
    closure(0, own // 4, 4, True, *step1)
    closure(own, 1, 2, True, *step1)
    closure(own + 2, 1, 1, False, *step1)
    kappa1 = kappas(low - 2, high + 2)
    ce1, cn1 = coefficients(kappa1, low - 1, high + 1)
    de1, dn1 = diffs(c1, low - 1, high + 1)
    c2 = diffuse(c1, ce1, cn1, de1, dn1, low, high)
    for i in range(low, high + 1):
        out_tracer[pl.ds(i - low, 8, stride=rows), :] = c2[i][0]
    lam2 = {}
    for i in range(low - 2, high + 3):
        lam2[i] = (tile_at(i, 1), unpack(side_l_packed, i))
    le, ln = diffs(lam2, low - 1, high + 1)
    direct = diffuse(lam2, ce1, cn1, le, ln, low - 1, high + 1)
    bars = kappa_bars(de1, dn1, le, ln, low - 1, high + 1)
    for i in range(low - 1, high + 2):
        d3_tiles[tile_of[i]] = bars[i][0]
    d3_tiles[side_tile] = pack({i: bars[i][1] for i in range(low, high + 1)})
    d3_tiles[rows + 3] = zero
    acc_w2[...] = jnp.zeros_like(acc_w2)
    acc_a1[...] = jnp.zeros_like(acc_a1)
    acc_head[...] = jnp.zeros_like(acc_head)
    closure_back(0, own // 4, 4, True, *step1[1:])
    closure_back(own, 1, 2, False, *step1[1:])
    side_bar = bar_tiles[side_tile]
    lam1 = {}
    for i in range(low - 1, high + 2):
        main = direct[i][0] + bar_tiles[tile_of[i]]
        side = direct[i][1] + unpack(side_bar, i)
        lam1[i] = (main, side)
    le, ln = diffs(lam1, low, high)
    direct = diffuse(lam1, ce0, cn0, le, ln, low, high)
    bars = kappa_bars(de0, dn0, le, ln, low, high)
    for i in range(low, high + 1):
        d3_tiles[tile_of[i]] = bars[i][0]
    closure_back(0, own // 4, 4, True, *step0[1:])
    for i in range(low, high + 1):
        out_grad[pl.ds(i - low, 8, stride=rows), :] = direct[i][0] + bar_tiles[tile_of[i]]
    first = [None] * 6

    def add(f, value):
        first[f] = value if first[f] is None else first[f] + value

    for k in range(DEPTH):
        cells = acc_a1[2 * HID * k : 2 * HID * k + HID, :]
        cells = cells + acc_a1[2 * HID * k + HID : 2 * HID * (k + 1), :]
        cells = jnp.concatenate([cells, jnp.zeros((HID, LANES - 32), F32)], 1)
        turned = jnp.transpose(cells)
        turned = turned[0:16] + turned[16:32]
        for t in range(2):
            add(t, turned[t * 4 + k : t * 4 + k + 1])
            if k >= 1:
                add(2 + t, -turned[8 + t * 4 + k - 1 : 8 + t * 4 + k])
            add(4 + t, turned[8 + t * 4 + k : 8 + t * 4 + k + 1])
    head = jnp.sum(jnp.transpose(acc_head[:, :LANES] + acc_head[:, LANES:]), 0, keepdims=True)
    rest = jnp.concatenate(first + [head, jnp.zeros_like(head)], 0)
    second = (acc_w2[:HID, :HID] + acc_w2[HID:, HID:]) + (acc_w2[:HID, HID:] + acc_w2[HID:, :HID])
    odd = jnp.bitwise_and(lax.axis_index("lat"), 1) == 1
    left, right = second[: HID // 2], second[HID // 2 :]
    out_keep[0 : HID // 2, :] = jnp.where(odd, right, left)
    out_give[0 : HID // 2, :] = jnp.where(odd, left, right)
    out_keep[HID // 2 :, :] = jnp.where(odd, 0.0, rest)
    out_give[HID // 2 :, :] = jnp.where(odd, rest, 0.0)


def finish_kernel(scale, mine, other, w1_out, w2_out, wh_out):
    odd = jnp.bitwise_and(lax.axis_index("lat"), 1) == 1
    half = HID // 2
    a, b = mine[...], other[...]
    left, right = jnp.where(odd, b, a) * scale, jnp.where(odd, a, b) * scale
    w2_out[0:half, :] = left[:half]
    w2_out[half:, :] = right[:half]
    w1_out[...] = left[half : half + 6]
    wh_out[...] = left[half + 6 : half + 7]


VMEM = pl.BlockSpec(memory_space=pltpu.VMEM)
SMEM = pl.BlockSpec(memory_space=pltpu.SMEM)
HBM = pl.BlockSpec(memory_space=pltpu.HBM)


def call(kernel, outs, ins, out_specs=None, scratch=(), limit=4 * 1024 * 1024, flops=1_000_000, size=1_000_000):
    return pl.pallas_call(
        kernel,
        out_shape=outs,
        in_specs=ins,
        out_specs=out_specs or [VMEM] * len(outs),
        scratch_shapes=list(scratch),
        compiler_params=pltpu.CompilerParams(vmem_limit_bytes=limit),
        cost_estimate=pl.CostEstimate(flops=flops, bytes_accessed=size, transcendentals=0),
    )


def shape(*dims, dtype=F32):
    return jax.ShapeDtypeStruct(dims, dtype)


def per_device(
    tracers,
    land_mask,
    level_counts,
    fold_partner,
    cotangent,
    w_first,
    b_first,
    w_second,
    b_second,
    w_head,
    b_head,
):
    rows, cols = land_mask.shape
    n_lon, n_lat = lax.axis_size("lon"), lax.axis_size("lat")
    tracer2 = tracers.reshape(8 * rows, cols)
    cot2 = cotangent.reshape(8 * rows, cols)

    args = (
        tracer2,
        cot2,
        land_mask,
        level_counts,
        fold_partner,
        w_first,
        b_first.reshape(1, HID),
        w_second,
        b_second.reshape(1, HID),
        w_head.reshape(1, HID),
        b_head,
    )
    spaces = [pltpu.SMEM if x is fold_partner or x is b_head else pltpu.VMEM for x in args]
    south_first, north, south_last, turn, offset, own_rows, a1, w2t, w2, cols_w = call(
        functools.partial(prepare_kernel, rows, cols),
        [shape(48, LANES)] * 3
        + [
            shape(1, dtype=jnp.int32),
            shape(8, LANES, dtype=jnp.int32),
            shape(24 * rows, LANES),
            shape(DEPTH * HID, 64, dtype=BF16),
            shape(2 * HID, 2 * HID, dtype=BF16),
            shape(2 * HID, 2 * HID, dtype=BF16),
            shape(8 * HID + 8, LANES),
        ],
        [HBM] * len(args),
        out_specs=[VMEM] * 3 + [SMEM] + [VMEM] * 6,
        limit=None,
        scratch=[space(x.shape, x.dtype) for space, x in zip(spaces, args)]
        + [pltpu.SemaphoreType.DMA((len(args),))],
    )(*args)

    def exchange(j, first, second, third):
        top = n_lat - 1

        def send(x, plain, fold):
            pairs = [
                (b * n_lat + source, b * n_lat + target)
                for b in range(n_lon)
                for source, target in plain
            ]
            if fold is not None:
                pairs += [
                    (b * n_lat + top, ((fold - b) % n_lon) * n_lat + top) for b in range(n_lon)
                ]
            return lax.ppermute(x, ("lon", "lat"), pairs)

        south = [(i + 1, i) for i in range(top - 1)] + [(0, top - 1)]
        north = [(i, i + 1) for i in range(top - 1)] + [(top - 1, 0)]
        last = [(i, i ^ 1) for i in range(n_lat)]
        return send(first, south, j), send(second, north, j - 1), send(third, last, None)

    from_first, from_second, from_third = lax.switch(
        turn[0],
        [functools.partial(exchange, j) for j in range(n_lon)],
        south_first,
        north,
        south_last,
    )

    total = rows + 2 * HALO
    halo_rows, packed = call(
        functools.partial(assemble_kernel, rows),
        [shape(24 * 2 * HALO, LANES), shape(24, LANES)],
        [VMEM] * 5,
    )(offset, from_first, from_second, from_third, own_rows)
    from_west = lax.ppermute(packed, "lon", [(i, (i + 1) % n_lon) for i in range(n_lon)])
    from_east = lax.ppermute(packed, "lon", [((i + 1) % n_lon, i) for i in range(n_lon)])

    n_tiles = total + 1 + (total + 1) % 2
    pairs0 = rows // 2
    pairs1 = rows // 2 + 2
    tiles = pltpu.VMEM((n_tiles, 8, LANES), F32)
    wide = 2 * LANES
    scratch = (
        [tiles] * 9
        + [pltpu.VMEM((n, 64, wide), BF16) for n in (pairs0, pairs1)]
        + [pltpu.VMEM((n, DEPTH, 2 * HID, wide), BF16) for n in (pairs0, pairs1)]
        + [pltpu.VMEM((n, DEPTH, HID, wide), F32) for n in (pairs0, pairs1)]
        + [pltpu.VMEM((n, DEPTH, HID, wide), F32) for n in (pairs0, pairs1)]
        + [
            pltpu.VMEM((2 * HID, 2 * HID), F32),
            pltpu.VMEM((DEPTH * 2 * HID, 32), F32),
            pltpu.VMEM((HID, wide), F32),
        ]
    )
    final, grad, keep, give = call(
        functools.partial(steps_kernel, rows),
        [shape(8 * rows, LANES)] * 2 + [shape(HID // 2 + 8, LANES)] * 2,
        [VMEM] * 8,
        scratch=scratch,
        limit=36 * 1024 * 1024,
        flops=10_000_000_000,
    )(own_rows, halo_rows, from_west, from_east, a1, w2t, w2, cols_w)

    def swap(x, mask):
        pairs = [(i, i ^ mask) for i in range(n_lon * n_lat)]
        return lax.ppermute(x, ("lon", "lat"), pairs)

    sums = keep + swap(give, 1)
    bits = [1 << b for b in range(1, (n_lon * n_lat).bit_length() - 1)]
    while bits:
        a, bits = bits[0], bits[1:]
        if bits:
            b, bits = bits[0], bits[1:]
            near, far, both = swap(sums, a), swap(sums, b), swap(sums, a | b)
            sums = (sums + near) + (far + both)
        else:
            sums = sums + swap(sums, a)
    other = swap(sums, 1)
    scale = 1.0 / math.sqrt(n_lon * cols * n_lat * rows * DEPTH)
    first_grad, second_grad, head_grad = call(
        functools.partial(finish_kernel, scale),
        [shape(6, HID), shape(HID, HID), shape(1, HID)],
        [VMEM] * 2,
    )(sums, other)
    return (
        final.reshape(tracers.shape),
        grad.reshape(tracers.shape),
        first_grad,
        second_grad,
        head_grad.reshape(HID),
    )


def solution(mesh):
    return jax.shard_map(
        per_device,
        mesh=mesh,
        in_specs=(
            P(None, None, "lat", "lon"),
            P("lat", "lon"),
            P("lat", "lon"),
            P("lon"),
            P(None, None, "lat", "lon"),
            P(),
            P(),
            P(),
            P(),
            P(),
            P(),
        ),
        out_specs=(P(None, None, "lat", "lon"), P(None, None, "lat", "lon"), P(), P(), P()),
        check_vma=False,
    )
```

time: 90.9 us -> 64.5 us (0.71)
  Pallas kernels: 42.7 us -> 22.6 us
  waiting for transfers between devices: 21.9 us -> 16.5 us
  local copies, waits for them, and re-layouts: 7.33 us -> 5.37 us
    pallas_call x4 -> x3, Pallas kernels: 41.1 us -> 22 us  [the longest x1 18.7 us: per_device(): call(functools.partial(steps_kernel, rows), [shape(8 * rows, LANES)] * 2...]
    ppermute x9 -> x11, waiting for transfers between devices: 17.8 us -> 10.1 us  [the longest x8 6.28 us: swap(): return lax.ppermute(x, ('lon', 'lat'), pairs)]
    ppermute x9 -> x11, starting transfers between devices: 10.8 us -> 13 us  [the longest x8 7.99 us: swap(): return lax.ppermute(x, ('lon', 'lat'), pairs)]
    unnamed x22 -> x14, local copies, waits for them, and re-layouts: 7.33 us -> 5.37 us
    ppermute x1, waiting for transfers between devices: 0.01 us -> 1.4 us  [per_device(): lax.ppermute(packed, 'lon', [((i + 1) % n_lon, i) for i in range(n_lon)])]
    ppermute x1, starting transfers between devices: 6 us -> 4.61 us  [per_device(): lax.ppermute(packed, 'lon', [((i + 1) % n_lon, i) for i in range(n_lon)])]
    pallas_call x1, Pallas kernels: 1.55 us -> 0.64 us  [per_device(): call(functools.partial(finish_kernel, scale), [shape(6, HID), shape(HID,...]
  transfers between devices with their start and end apart: 11 -> 13, of which waited for: 6 -> 10; matrix products, arithmetic and copies ran while one was open for 0% -> 0% of each run, Pallas kernels for 2% -> 0%
where the time goes in v1:
time: 64.5 us; the launch traced here: 64.1 us
  Pallas kernels  22.6 us (35%)
  starting transfers between devices  17.6 us (27%)
  waiting for transfers between devices  16.5 us (26%)
  local copies, waits for them, and re-layouts  5.37 us (8%)
  between operations  1.99 us (3%)
    pallas_call x1, Pallas kernels, per_device(): call(functools.partial(steps_kernel, rows), [shape(8 * rows, LANES)] * 2...  18.7 us
    ppermute x8, starting transfers between devices, swap(): return lax.ppermute(x, ('lon', 'lat'), pairs)  7.99 us
    ppermute x8, waiting for transfers between devices, swap(): return lax.ppermute(x, ('lon', 'lat'), pairs)  6.28 us
    unnamed x14, local copies, waits for them, and re-layouts  5.37 us
    ppermute x3, starting transfers between devices, send(): return lax.ppermute(x, ('lon', 'lat'), pairs)  5.03 us
    ppermute x1, waiting for transfers between devices, per_device(): lax.ppermute(packed, 'lon', [(i, (i + 1) % n_lon) for i in range(n_lon)])  4.99 us
    ppermute x1, starting transfers between devices, per_device(): lax.ppermute(packed, 'lon', [((i + 1) % n_lon, i) for i in range(n_lon)])  4.61 us
    ppermute x3, waiting for transfers between devices, send(): return lax.ppermute(x, ('lon', 'lat'), pairs)  3.81 us
  transfers between devices with their start and end apart: 13, of which 10 were waited for; matrix products, arithmetic and copies ran while one was open for 0% of the time, Pallas kernels for 0%

profile of v1, /device:TPU:0, one launch (start us, length us, event | category | flops | bytes accessed | tf_op | source)
XLA Modules:
  0.0 64.1 jit_solution(15252125832197872084)
XLA Ops:
  1.3 2.3 %shard_map.146 = (f32[48,128]{1,0:T(8,128)S(1)}, f32[48,128]{1,0:T(8,128)S(1)}, f32[48,128]{1,0:T(8,128)S(1)}, s32[1]{0:T(128)}, s32[8,128]{1,0:T(8,128)}, /*ind...) custom-call(f32[128,128]{1,0:T(8,128)} %bitcast.9, ...), custom_call_target="tpu_custom_call" | custom-call | flops 1000000 | bytes 1000000 | tf_op jit(solution)/shard_map/pallas_call | solution.py:683
  4.2 8.9 %conditional.1 = (f32[48,128]{1,0:T(8,128)}, f32[48,128]{1,0:T(8,128)}, f32[48,128]{1,0:T(8,128)}) conditional(s32[]{:T(128)} %bitcast.5, (f32[48,128]{1,0:T(8,128)S(1)}, f32[48,128]{1,0:T(8,128)S(1)}, f32[48,128]{1,0:T(8,128)S(1)}) %tuple.40, (f32[48,128]{1,0:T(8,128)S(1)}, f32[48,128]{1,0:T(8,128)S(1)}, ...), branch_computations={%region_0.0_spmd, %region_1.0_spmd, %region_2.0_spmd, %region_3.0_... | conditional | bytes 295056 | solution.py:722
  4.3 4.8 %collective-permute-start.18 = (f32[48,128]{1,0:T(8,128)S(1)}, f32[48,128]{1,0:T(8,128)}, u32[]{:S(2)}, u32[]{:S(2)}) collective-permute-start(f32[48,128]{1,0:T(8,128)S(1)} %get-tuple-element.66), channel_id=1, source_target_pairs={{1,0},{2,1},{0,2},{5,4},{6,5},{4,6},{9,8},{10,9},{8,10},{13,12},{1... | collective-permute-start | bytes 73736 | tf_op jit(solution)/shard_map/cond/branch_6_fun/ppermute | solution.py:715
  9.1 0.1 collective-permute-start.19
  9.2 0.1 collective-permute-start.20
  9.3 1.3 %collective-permute-done.18 = f32[48,128]{1,0:T(8,128)} collective-permute-done((f32[48,128]{1,0:T(8,128)S(1)}, f32[48,128]{1,0:T(8,128)}, u32[]{:S(2)}, u32[]{:S(2)}) %collective-permute-start.18) | collective-permute-done | bytes 24608 | tf_op jit(solution)/shard_map/cond/branch_6_fun/ppermute | solution.py:715
  10.6 2.5 %collective-permute-done.19 = f32[48,128]{1,0:T(8,128)} collective-permute-done((f32[48,128]{1,0:T(8,128)S(1)}, f32[48,128]{1,0:T(8,128)}, u32[]{:S(2)}, u32[]{:S(2)}) %collective-permute-start.19) | collective-permute-done | bytes 24608 | tf_op jit(solution)/shard_map/cond/branch_6_fun/ppermute | solution.py:715
  13.1 0.0 collective-permute-done.20
  13.1 0.0 copy-start.2
  13.1 0.7 %copy-done.2 = s32[8,128]{1,0:T(8,128)S(1)} copy-done((s32[8,128]{1,0:T(8,128)S(1)}, s32[8,128]{1,0:T(8,128)}, u32[]{:S(2)}) %copy-start.2) | copy-done | bytes 4120
  13.8 0.0 copy-start
  13.8 0.9 %copy-done = f32[384,128]{1,0:T(8,128)S(1)} copy-done((f32[384,128]{1,0:T(8,128)S(1)}, f32[384,128]{1,0:T(8,128)}, u32[]{:S(2)}) %copy-start) | copy-done | bytes 196632
  14.7 0.0 copy-start.1
  14.7 1.0 %shard_map.147 = (f32[144,128]{1,0:T(8,128)S(1)}, f32[24,128]{1,0:T(8,128)S(1)}) custom-call(s32[8,128]{1,0:T(8,128)S(1)} %copy-done.2, f32[48,128]{1,0:T(8,128)} %get-tuple-element.105.first, f32[48,128]{1,0:T(8,128)} %get-tuple-element.106.second, f32[48,128]{1,0:T(8,128)} %get-tuple-element.107.third, f32[384,128]{1,0:T(8,128)S(1)} %copy-done), custom_call_target="tpu_custom_call" | custom-call | flops 1000000 | bytes 1000000 | tf_op jit(solution)/shard_map/pallas_call | solution.py:731
  15.7 4.6 %collective-permute-start.25 = (f32[24,128]{1,0:T(8,128)S(1)}, f32[24,128]{1,0:T(8,128)S(1)}, u32[]{:S(2)}, u32[]{:S(2)}) collective-permute-start(f32[24,128]{1,0:T(8,128)S(1)} %get-tuple-element.109), channel_id=1, source_target_pairs={{4,0},{8,4},{12,8},{16,12},{20,16},{24,20},{28,24},{0,28},{5,1},{9... | collective-permute-start | bytes 36872 | tf_op jit(solution)/shard_map/ppermute | solution.py:737
  20.3 0.0 collective-permute-start.24
  20.3 1.4 %collective-permute-done.25.east_in = f32[24,128]{1,0:T(8,128)S(1)} collective-permute-done((f32[24,128]{1,0:T(8,128)S(1)}, f32[24,128]{1,0:T(8,128)S(1)}, u32[]{:S(2)}, u32[]{:S(2)}) %collective-permute-start.25) | collective-permute-done | bytes 12320 | tf_op jit(solution)/shard_map/ppermute | solution.py:737
  21.7 5.0 %collective-permute-done.24.west_in = f32[24,128]{1,0:T(8,128)S(1)} collective-permute-done((f32[24,128]{1,0:T(8,128)S(1)}, f32[24,128]{1,0:T(8,128)S(1)}, u32[]{:S(2)}, u32[]{:S(2)}) %collective-permute-start.24) | collective-permute-done | bytes 12320 | tf_op jit(solution)/shard_map/ppermute | solution.py:736
  26.7 0.0 copy-done.1
  26.7 0.0 copy-start.3
  26.7 1.0 %copy-done.3 = f32[1032,128]{1,0:T(8,128)S(1)} copy-done((f32[1032,128]{1,0:T(8,128)S(1)}, f32[1032,128]{1,0:T(8,128)}, u32[]{:S(2)}) %copy-start.3) | copy-done | bytes 528408
  27.7 0.0 copy-start.4
  27.7 0.9 %copy-done.4 = bf16[512,64]{1,0:T(8,128)(2,1)S(1)} copy-done((bf16[512,64]{1,0:T(8,128)(2,1)S(1)}, bf16[512,64]{1,0:T(8,128)(2,1)}, u32[]{:S(2)}) %copy-start.4) | copy-done | bytes 65560
  28.6 0.0 copy-start.5
  28.6 0.9 %copy-done.5 = bf16[256,256]{1,0:T(8,128)(2,1)S(1)} copy-done((bf16[256,256]{1,0:T(8,128)(2,1)S(1)}, bf16[256,256]{1,0:T(8,128)(2,1)}, u32[]{:S(2)}) %copy-start.5) | copy-done | bytes 131096
  29.5 0.0 copy-start.6
  29.5 0.9 %copy-done.6 = bf16[256,256]{1,0:T(8,128)(2,1)S(1)} copy-done((bf16[256,256]{1,0:T(8,128)(2,1)S(1)}, bf16[256,256]{1,0:T(8,128)(2,1)}, u32[]{:S(2)}) %copy-start.6) | copy-done | bytes 131096
  30.4 18.7 %shard_map.148 = (f32[128,128]{1,0:T(8,128)}, f32[128,128]{1,0:T(8,128)}, f32[72,128]{1,0:T(8,128)S(1)}, f32[72,128]{1,0:T(8,128)S(1)}) custom-call(f32[384,128]{1,0:T(8,128)S(1)} %copy-done.1, f32[144,128]{1,0:T(8,128)S(1)} %get-tuple-element.108.halo_rows, f32[24,128]{1,0:T(8,128)S(1)} %collective-permute-done.24.west_in, ...), custom_call_target="tpu_custom_call" | custom-call | flops 10000000000 | bytes 1000000 | tf_op jit(solution)/shard_map/pallas_call | solution.py:756
  49.1 0.0 collective-permute-start.26
  49.2 1.2 %collective-permute-done.26 = f32[72,128]{1,0:T(8,128)S(1)} collective-permute-done((f32[72,128]{1,0:T(8,128)S(1)}, f32[72,128]{1,0:T(8,128)S(1)}, u32[]{:S(2)}, u32[]{:S(2)}) %collective-permute-start.26) | collective-permute-done | bytes 36896 | tf_op jit(solution)/shard_map/ppermute | solution.py:767
  50.4 0.0 collective-permute-start.29
  50.4 1.4 %collective-permute-start.28 = (f32[72,128]{1,0:T(8,128)S(1)}, f32[72,128]{1,0:T(8,128)S(1)}, u32[]{:S(2)}, u32[]{:S(2)}) collective-permute-start(f32[72,128]{1,0:T(8,128)S(1)} %add.21), channel_id=1, source_target_pairs={{0,4},{1,5},{2,6},{3,7},{4,0},{5,1},{6,2},{7,3},{8,12},{9,13},{10,... | collective-permute-start | bytes 110600 | tf_op jit(solution)/shard_map/ppermute | solution.py:767
  51.8 2.1 %collective-permute-start.27 = (f32[72,128]{1,0:T(8,128)S(1)}, f32[72,128]{1,0:T(8,128)S(1)}, u32[]{:S(2)}, u32[]{:S(2)}) collective-permute-start(f32[72,128]{1,0:T(8,128)S(1)} %add.21), channel_id=1, source_target_pairs={{0,2},{1,3},{2,0},{3,1},{4,6},{5,7},{6,4},{7,5},{8,10},{9,11},{10,... | collective-permute-start | bytes 110600 | tf_op jit(solution)/shard_map/ppermute | solution.py:767
  53.9 1.4 %collective-permute-done.29 = f32[72,128]{1,0:T(8,128)S(1)} collective-permute-done((f32[72,128]{1,0:T(8,128)S(1)}, f32[72,128]{1,0:T(8,128)S(1)}, u32[]{:S(2)}, u32[]{:S(2)}) %collective-permute-start.29) | collective-permute-done | bytes 36896 | tf_op jit(solution)/shard_map/ppermute | solution.py:767
  55.2 0.0 collective-permute-done.28
  55.2 0.6 collective-permute-done.27
  55.8 0.1 collective-permute-start.32
  55.9 0.1 collective-permute-start.31
  56.0 4.3 %collective-permute-start.30 = (f32[72,128]{1,0:T(8,128)S(1)}, f32[72,128]{1,0:T(8,128)S(1)}, u32[]{:S(2)}, u32[]{:S(2)}) collective-permute-start(f32[72,128]{1,0:T(8,128)S(1)} %add_add_fusion.1), channel_id=1, source_target_pairs={{0,8},{1,9},{2,10},{3,11},{4,12},{5,13},{6,14},{7,15},{8,0},{9,1},... | collective-permute-start | bytes 110600 | tf_op jit(solution)/shard_map/ppermute | solution.py:767
  60.3 1.4 %collective-permute-done.32 = f32[72,128]{1,0:T(8,128)S(1)} collective-permute-done((f32[72,128]{1,0:T(8,128)S(1)}, f32[72,128]{1,0:T(8,128)S(1)}, u32[]{:S(2)}, u32[]{:S(2)}) %collective-permute-start.32) | collective-permute-done | bytes 36896 | tf_op jit(solution)/shard_map/ppermute | solution.py:767
  61.6 0.0 collective-permute-done.31
  61.6 0.6 collective-permute-done.30
  62.2 0.1 collective-permute-start.33
  62.3 1.2 %collective-permute-done.33.other = f32[72,128]{1,0:T(8,128)S(1)} collective-permute-done((f32[72,128]{1,0:T(8,128)S(1)}, f32[72,128]{1,0:T(8,128)S(1)}, u32[]{:S(2)}, u32[]{:S(2)}) %collective-permute-start.33) | collective-permute-done | bytes 36896 | tf_op jit(solution)/shard_map/ppermute | solution.py:767
  63.5 0.6 shard_map.149
  (3 shorter events, 0.0 us)
Async XLA Ops:
  4.3 6.4 %collective-permute-start.18 = (f32[48,128]{1,0:T(8,128)S(1)}, f32[48,128]{1,0:T(8,128)}, u32[]{:S(2)}, u32[]{:S(2)}) collective-permute-start(f32[48,128]{1,0:T(8,128)S(1)} %get-tuple-element.66), channel_id=1, source_target_pairs={{1,0},{2,1},{0,2},{5,4},{6,5},{4,6},{9,8},{10,9},{8,10},{13,12},{1... | collective-permute-start | bytes 73736 | tf_op jit(solution)/shard_map/cond/branch_6_fun/ppermute | solution.py:715
  9.1 4.0 %collective-permute-start.19 = (f32[48,128]{1,0:T(8,128)S(1)}, f32[48,128]{1,0:T(8,128)}, u32[]{:S(2)}, u32[]{:S(2)}) collective-permute-start(f32[48,128]{1,0:T(8,128)S(1)} %get-tuple-element.67), channel_id=1, source_target_pairs={{0,1},{1,2},{2,0},{4,5},{5,6},{6,4},{8,9},{9,10},{10,8},{12,13},{1... | collective-permute-start | bytes 73736 | tf_op jit(solution)/shard_map/cond/branch_6_fun/ppermute | solution.py:715
  9.2 3.9 %collective-permute-start.20 = (f32[48,128]{1,0:T(8,128)S(1)}, f32[48,128]{1,0:T(8,128)}, u32[]{:S(2)}, u32[]{:S(2)}) collective-permute-start(f32[48,128]{1,0:T(8,128)S(1)} %get-tuple-element.68), channel_id=1, source_target_pairs={{0,1},{1,0},{2,3},{3,2},{4,5},{5,4},{6,7},{7,6},{8,9},{9,8},{10,11... | collective-permute-start | bytes 73736 | tf_op jit(solution)/shard_map/cond/branch_6_fun/ppermute | solution.py:715
  13.1 0.7 %copy-start.2 = (s32[8,128]{1,0:T(8,128)S(1)}, s32[8,128]{1,0:T(8,128)}, u32[]{:S(2)}) copy-start(s32[8,128]{1,0:T(8,128)} %get-tuple-element.100.offset_in) | copy-start | bytes 12292
  13.8 0.9 %copy-start = (f32[384,128]{1,0:T(8,128)S(1)}, f32[384,128]{1,0:T(8,128)}, u32[]{:S(2)}) copy-start(f32[384,128]{1,0:T(8,128)} %get-tuple-element.99.own.own_rows) | copy-start | bytes 589828
  14.7 12.0 %copy-start.1 = (f32[384,128]{1,0:T(8,128)S(1)}, f32[384,128]{1,0:T(8,128)}, u32[]{:S(2)}) copy-start(f32[384,128]{1,0:T(8,128)} %get-tuple-element.99.own.own_rows) | copy-start | bytes 589828
  15.7 6.0 %collective-permute-start.25 = (f32[24,128]{1,0:T(8,128)S(1)}, f32[24,128]{1,0:T(8,128)S(1)}, u32[]{:S(2)}, u32[]{:S(2)}) collective-permute-start(f32[24,128]{1,0:T(8,128)S(1)} %get-tuple-element.109), channel_id=1, source_target_pairs={{4,0},{8,4},{12,8},{16,12},{20,16},{24,20},{28,24},{0,28},{5,1},{9... | collective-permute-start | bytes 36872 | tf_op jit(solution)/shard_map/ppermute | solution.py:737
  20.3 6.4 %collective-permute-start.24 = (f32[24,128]{1,0:T(8,128)S(1)}, f32[24,128]{1,0:T(8,128)S(1)}, u32[]{:S(2)}, u32[]{:S(2)}) collective-permute-start(f32[24,128]{1,0:T(8,128)S(1)} %get-tuple-element.109), channel_id=1, source_target_pairs={{0,4},{4,8},{8,12},{12,16},{16,20},{20,24},{24,28},{28,0},{1,5},{5... | collective-permute-start | bytes 36872 | tf_op jit(solution)/shard_map/ppermute | solution.py:736
  26.7 1.0 %copy-start.3 = (f32[1032,128]{1,0:T(8,128)S(1)}, f32[1032,128]{1,0:T(8,128)}, u32[]{:S(2)}) copy-start(f32[1032,128]{1,0:T(8,128)} %get-tuple-element.113.cols) | copy-start | bytes 1585156
  27.7 0.9 %copy-start.4 = (bf16[512,64]{1,0:T(8,128)(2,1)S(1)}, bf16[512,64]{1,0:T(8,128)(2,1)}, u32[]{:S(2)}) copy-start(bf16[512,64]{1,0:T(8,128)(2,1)} %get-tuple-element.110.a1) | copy-start | bytes 196612
  28.6 0.9 %copy-start.5 = (bf16[256,256]{1,0:T(8,128)(2,1)S(1)}, bf16[256,256]{1,0:T(8,128)(2,1)}, u32[]{:S(2)}) copy-start(bf16[256,256]{1,0:T(8,128)(2,1)} %get-tuple-element.111.w2t) | copy-start | bytes 393220
  29.5 0.9 %copy-start.6 = (bf16[256,256]{1,0:T(8,128)(2,1)S(1)}, bf16[256,256]{1,0:T(8,128)(2,1)}, u32[]{:S(2)}) copy-start(bf16[256,256]{1,0:T(8,128)(2,1)} %get-tuple-element.112.w2) | copy-start | bytes 393220
  49.1 1.2 %collective-permute-start.26 = (f32[72,128]{1,0:T(8,128)S(1)}, f32[72,128]{1,0:T(8,128)S(1)}, u32[]{:S(2)}, u32[]{:S(2)}) collective-permute-start(f32[72,128]{1,0:T(8,128)S(1)} %get-tuple-element.117), channel_id=1, source_target_pairs={{0,1},{1,0},{2,3},{3,2},{4,5},{5,4},{6,7},{7,6},{8,9},{9,8},{10,11... | collective-permute-start | bytes 110600 | tf_op jit(solution)/shard_map/ppermute | solution.py:767
  50.4 4.9 %collective-permute-start.29 = (f32[72,128]{1,0:T(8,128)S(1)}, f32[72,128]{1,0:T(8,128)S(1)}, u32[]{:S(2)}, u32[]{:S(2)}) collective-permute-start(f32[72,128]{1,0:T(8,128)S(1)} %add.21), channel_id=1, source_target_pairs={{0,6},{1,7},{2,4},{3,5},{4,2},{5,3},{6,0},{7,1},{8,14},{9,15},{10,... | collective-permute-start | bytes 110600 | tf_op jit(solution)/shard_map/ppermute | solution.py:767
  50.4 4.9 %collective-permute-start.28 = (f32[72,128]{1,0:T(8,128)S(1)}, f32[72,128]{1,0:T(8,128)S(1)}, u32[]{:S(2)}, u32[]{:S(2)}) collective-permute-start(f32[72,128]{1,0:T(8,128)S(1)} %add.21), channel_id=1, source_target_pairs={{0,4},{1,5},{2,6},{3,7},{4,0},{5,1},{6,2},{7,3},{8,12},{9,13},{10,... | collective-permute-start | bytes 110600 | tf_op jit(solution)/shard_map/ppermute | solution.py:767
  51.8 4.0 %collective-permute-start.27 = (f32[72,128]{1,0:T(8,128)S(1)}, f32[72,128]{1,0:T(8,128)S(1)}, u32[]{:S(2)}, u32[]{:S(2)}) collective-permute-start(f32[72,128]{1,0:T(8,128)S(1)} %add.21), channel_id=1, source_target_pairs={{0,2},{1,3},{2,0},{3,1},{4,6},{5,7},{6,4},{7,5},{8,10},{9,11},{10,... | collective-permute-start | bytes 110600 | tf_op jit(solution)/shard_map/ppermute | solution.py:767
  55.8 5.8 %collective-permute-start.32 = (f32[72,128]{1,0:T(8,128)S(1)}, f32[72,128]{1,0:T(8,128)S(1)}, u32[]{:S(2)}, u32[]{:S(2)}) collective-permute-start(f32[72,128]{1,0:T(8,128)S(1)} %add_add_fusion.1), channel_id=1, source_target_pairs={{0,24},{1,25},{2,26},{3,27},{4,28},{5,29},{6,30},{7,31},{8,16},{9,... | collective-permute-start | bytes 110600 | tf_op jit(solution)/shard_map/ppermute | solution.py:767
  55.9 5.7 %collective-permute-start.31 = (f32[72,128]{1,0:T(8,128)S(1)}, f32[72,128]{1,0:T(8,128)S(1)}, u32[]{:S(2)}, u32[]{:S(2)}) collective-permute-start(f32[72,128]{1,0:T(8,128)S(1)} %add_add_fusion.1), channel_id=1, source_target_pairs={{0,16},{1,17},{2,18},{3,19},{4,20},{5,21},{6,22},{7,23},{8,24},{9,... | collective-permute-start | bytes 110600 | tf_op jit(solution)/shard_map/ppermute | solution.py:767
  56.0 6.2 %collective-permute-start.30 = (f32[72,128]{1,0:T(8,128)S(1)}, f32[72,128]{1,0:T(8,128)S(1)}, u32[]{:S(2)}, u32[]{:S(2)}) collective-permute-start(f32[72,128]{1,0:T(8,128)S(1)} %add_add_fusion.1), channel_id=1, source_target_pairs={{0,8},{1,9},{2,10},{3,11},{4,12},{5,13},{6,14},{7,15},{8,0},{9,1},... | collective-permute-start | bytes 110600 | tf_op jit(solution)/shard_map/ppermute | solution.py:767
  62.2 1.3 %collective-permute-start.33 = (f32[72,128]{1,0:T(8,128)S(1)}, f32[72,128]{1,0:T(8,128)S(1)}, u32[]{:S(2)}, u32[]{:S(2)}) collective-permute-start(f32[72,128]{1,0:T(8,128)S(1)} %add_add_fusion.mine), channel_id=1, source_target_pairs={{0,1},{1,0},{2,3},{3,2},{4,5},{5,4},{6,7},{7,6},{8,9},{9,8},{10,11... | collective-permute-start | bytes 110600 | tf_op jit(solution)/shard_map/ppermute | solution.py:767

commit v2 on v1

--- a/solution.py
+++ b/solution.py
@@ -28,7 +28,7 @@
     return lax.broadcasted_iota(jnp.int32, shape, dim)
 
 
-def prepare_kernel(
+def edges_kernel(
     rows,
     cols,
     tracer_hbm,
@@ -36,68 +36,36 @@
     land_hbm,
     levels_hbm,
     partner_hbm,
-    w1_hbm,
-    b1_hbm,
-    w2_hbm,
-    b2_hbm,
-    wh_hbm,
-    bh_hbm,
     south_first,
     north,
     south_last,
     turn_out,
-    offset_out,
-    own_out,
-    a1_out,
-    w2t_out,
-    w2_out,
-    col_out,
     tracer,
     cot,
     land,
     levels,
     partner,
-    w1,
-    b1,
-    w2,
-    b2,
-    wh,
-    bh,
     sems,
 ):
+    pairs = (
+        (partner_hbm, partner),
+        (tracer_hbm, tracer),
+        (cot_hbm, cot),
+        (land_hbm, land),
+        (levels_hbm, levels),
+    )
     copies = [
         pltpu.make_async_copy(source, target, sems.at[n])
-        for n, (source, target) in enumerate(
-            (
-                (partner_hbm, partner),
-                (tracer_hbm, tracer),
-                (cot_hbm, cot),
-                (land_hbm, land),
-                (levels_hbm, levels),
-                (w1_hbm, w1),
-                (b1_hbm, b1),
-                (w2_hbm, w2),
-                (b2_hbm, b2),
-                (wh_hbm, wh),
-                (bh_hbm, bh),
-            )
-        )
+        for n, (source, target) in enumerate(pairs)
     ]
     for copy in copies:
         copy.start()
     for copy in copies:
         copy.wait()
-    here = partner[0]
-    n_lon = lax.axis_size("lon")
-    turn_out[0] = lax.rem(lax.div(here, cols) + lax.axis_index("lon"), n_lon)
-    offset_out[...] = jnp.full((8, LANES), lax.rem(here, cols), jnp.int32)
+    turn_out[0] = lax.rem(lax.div(partner[0], cols) + lax.axis_index("lon"), lax.axis_size("lon"))
 
     at_top = lax.axis_index("lat") == lax.axis_size("lat") - 1
     depth = (land[...] * levels[...]).astype(F32)
-    for r in range(rows):
-        own_out[24 * r : 24 * r + 8, :] = tracer[pl.ds(r, 8, stride=rows), :]
-        own_out[24 * r + 8 : 24 * r + 16, :] = cot[pl.ds(r, 8, stride=rows), :]
-        own_out[24 * r + 16 : 24 * r + 24, :] = jnp.broadcast_to(depth[r : r + 1], (8, LANES))
 
     def edge(first, skip):
         parts = [tracer[pl.ds(first + j, 8, stride=rows), :] for j in range(HALO)]
@@ -109,10 +77,9 @@
     south_first[...] = jnp.where(at_top, high, low)
     north[...] = high
     south_last[...] = jnp.where(at_top, low, high)
-    prepare_weights(w1, b1, w2, b2, wh, bh, a1_out, w2t_out, w2_out, col_out)
-
-
-def prepare_weights(w1, b1, w2, b2, wh, bh, a1_out, w2t_out, w2_out, col_out):
+
+
+def weights_kernel(w1, b1, w2, b2, wh, bh, a1_out, w2t_out, w2_out, col_out):
     first = w1[...]
     bias_high, bias_low = split(b1[...])
     row = iota((16, LANES), 0)
@@ -142,17 +109,19 @@
     for n, vector in enumerate(vectors):
         column = jnp.transpose(jnp.broadcast_to(vector, (HID, LANES)))
         col_out[n * HID : (n + 1) * HID, :] = column
-    col_out[8 * HID : 8 * HID + 8, :] = jnp.full((8, LANES), bh[0], F32)
-
-
-def assemble_kernel(rows, offset_in, first, second, third, own, halo, packed):
+    col_out[8 * HID : 8 * HID + 8, :] = jnp.broadcast_to(bh[...], (8, LANES))
+
+
+def assemble_kernel(
+    rows, partner, first, second, third, tracer, cot, land, levels, ext, packed
+):
     lane = iota((8, LANES), 1)
     lat, n_lat = lax.axis_index("lat"), lax.axis_size("lat")
     at_top = lat == n_lat - 1
     below_top = lat == n_lat - 2
     at_bottom = lat == 0
-    offset = offset_in[...]
-    source = jnp.bitwise_and(offset - lane, LANES - 1)
+    source = jnp.broadcast_to(jnp.bitwise_and(partner[...], LANES - 1), (8, LANES))
+    offset = jnp.broadcast_to(source[:, 0:1], (8, LANES))
 
     def mirrored(place):
         both = jnp.where(
@@ -175,6 +144,7 @@
     def spread(tile, j):
         return jnp.broadcast_to(tile[j : j + 1], (8, LANES))
 
+    depth_here = (land[...] * levels[...]).astype(F32)
     depth_south = from_south(40)
     depth_north = from_north(40)
     depth_fold = mirrored(40)
@@ -187,19 +157,17 @@
             tile_l = from_south(24 + 8 * (i - 1)) if i >= 1 else zero
             tile_n = spread(depth_south, i)
         elif r < rows:
-            tile_c = own[24 * r : 24 * r + 8, :]
-            tile_l = own[24 * r + 8 : 24 * r + 16, :]
-            tile_n = own[24 * r + 16 : 24 * r + 24, :]
+            tile_c = tracer[pl.ds(r, 8, stride=rows), :]
+            tile_l = cot[pl.ds(r, 8, stride=rows), :]
+            tile_n = spread(depth_here, r)
         else:
             j = r - rows
             tile_c = north(8 * j, 8 * (2 - j))
             tile_l = north(24 + 8 * j, 24 + 8 * (1 - j)) if j < 2 else zero
             tile_n = jnp.where(at_top, spread(depth_fold, 2 - j), spread(depth_north, j))
         tiles.append((tile_c, tile_l, tile_n))
-        place = 24 * (i if r < 0 else i - rows)
-        if not 0 <= r < rows:
-            for part, tile in enumerate(tiles[-1]):
-                halo[place + 8 * part : place + 8 * part + 8, :] = tile
+        for part, tile in enumerate(tiles[-1]):
+            ext[24 * i + 8 * part : 24 * i + 8 * part + 8, :] = tile
     for part in range(3):
         acc = zero
         for slot in range(rows + 4):
@@ -211,8 +179,7 @@
 
 def steps_kernel(
     rows,
-    own_rows,
-    halo_rows,
+    ext,
     west_in,
     east_in,
     a1,
@@ -310,11 +277,8 @@
         return jnp.where(inside, 1.0, 0.0)
 
     def tile_at(i, part):
-        if HALO <= i < rows + HALO:
-            place = 24 * (i - HALO) + 8 * part
-            return own_rows[place : place + 8, :]
-        place = 24 * (i if i < HALO else i - rows) + 8 * part
-        return halo_rows[place : place + 8, :]
+        place = 24 * i + 8 * part
+        return ext[place : place + 8, :]
 
     c0, wet = {}, {}
     for i in range(total):
@@ -666,37 +630,16 @@
     tracer2 = tracers.reshape(8 * rows, cols)
     cot2 = cotangent.reshape(8 * rows, cols)
 
-    args = (
-        tracer2,
-        cot2,
-        land_mask,
-        level_counts,
-        fold_partner,
-        w_first,
-        b_first.reshape(1, HID),
-        w_second,
-        b_second.reshape(1, HID),
-        w_head.reshape(1, HID),
-        b_head,
-    )
-    spaces = [pltpu.SMEM if x is fold_partner or x is b_head else pltpu.VMEM for x in args]
-    south_first, north, south_last, turn, offset, own_rows, a1, w2t, w2, cols_w = call(
-        functools.partial(prepare_kernel, rows, cols),
-        [shape(48, LANES)] * 3
-        + [
-            shape(1, dtype=jnp.int32),
-            shape(8, LANES, dtype=jnp.int32),
-            shape(24 * rows, LANES),
-            shape(DEPTH * HID, 64, dtype=BF16),
-            shape(2 * HID, 2 * HID, dtype=BF16),
-            shape(2 * HID, 2 * HID, dtype=BF16),
-            shape(8 * HID + 8, LANES),
-        ],
+    args = (tracer2, cot2, land_mask, level_counts, fold_partner)
+    south_first, north, south_last, turn = call(
+        functools.partial(edges_kernel, rows, cols),
+        [shape(48, LANES)] * 3 + [shape(1, dtype=jnp.int32)],
         [HBM] * len(args),
-        out_specs=[VMEM] * 3 + [SMEM] + [VMEM] * 6,
+        out_specs=[VMEM] * 3 + [SMEM],
+        scratch=[pltpu.VMEM(x.shape, x.dtype) for x in args[:4]]
+        + [pltpu.SMEM(fold_partner.shape, fold_partner.dtype)]
+        + [pltpu.SemaphoreType.DMA((len(args),))],
         limit=None,
-        scratch=[space(x.shape, x.dtype) for space, x in zip(spaces, args)]
-        + [pltpu.SemaphoreType.DMA((len(args),))],
     )(*args)
 
     def exchange(j, first, second, third):
@@ -728,11 +671,37 @@
     )
 
     total = rows + 2 * HALO
-    halo_rows, packed = call(
+    ext, packed = call(
         functools.partial(assemble_kernel, rows),
-        [shape(24 * 2 * HALO, LANES), shape(24, LANES)],
-        [VMEM] * 5,
-    )(offset, from_first, from_second, from_third, own_rows)
+        [shape(24 * total, LANES), shape(24, LANES)],
+        [VMEM] * 8,
+    )(
+        fold_partner.reshape(1, cols),
+        from_first,
+        from_second,
+        from_third,
+        tracer2,
+        cot2,
+        land_mask,
+        level_counts,
+    )
+    a1, w2t, w2, cols_w = call(
+        weights_kernel,
+        [
+            shape(DEPTH * HID, 64, dtype=BF16),
+            shape(2 * HID, 2 * HID, dtype=BF16),
+            shape(2 * HID, 2 * HID, dtype=BF16),
+            shape(8 * HID + 8, LANES),
+        ],
+        [VMEM] * 6,
+    )(
+        w_first,
+        b_first.reshape(1, HID),
+        w_second,
+        b_second.reshape(1, HID),
+        w_head.reshape(1, HID),
+        b_head.reshape(1, 1),
+    )
     from_west = lax.ppermute(packed, "lon", [(i, (i + 1) % n_lon) for i in range(n_lon)])
     from_east = lax.ppermute(packed, "lon", [((i + 1) % n_lon, i) for i in range(n_lon)])
 
@@ -756,11 +725,11 @@
     final, grad, keep, give = call(
         functools.partial(steps_kernel, rows),
         [shape(8 * rows, LANES)] * 2 + [shape(HID // 2 + 8, LANES)] * 2,
-        [VMEM] * 8,
+        [VMEM] * 7,
         scratch=scratch,
         limit=36 * 1024 * 1024,
         flops=10_000_000_000,
-    )(own_rows, halo_rows, from_west, from_east, a1, w2t, w2, cols_w)
+    )(ext, from_west, from_east, a1, w2t, w2, cols_w)
 
     def swap(x, mask):
         pairs = [(i, i ^ mask) for i in range(n_lon * n_lat)]

time: 64.5 us -> 59.8 us (0.927)
  local copies, waits for them, and re-layouts: 5.37 us -> 1.31 us
  waiting for transfers between devices: 16.5 us -> 14.7 us
  Pallas kernels: 22.6 us -> 23.5 us
    unnamed x14 -> x20, local copies, waits for them, and re-layouts: 5.37 us -> 1.31 us
    ppermute x1, waiting for transfers between devices: 1.4 us -> 0.01 us  [per_device(): lax.ppermute(packed, 'lon', [((i + 1) % n_lon, i) for i in range(n_lon)])]
    pallas_call x1, Pallas kernels: 18.7 us -> 20.1 us  [per_device(): call(functools.partial(steps_kernel, rows), [shape(8 * rows, LANES)] * 2...]
    pallas_call x2 -> x3, Pallas kernels: 3.25 us -> 2.77 us  [the longest x1 1.49 us: per_device(): call(functools.partial(edges_kernel, rows, cols), [shape(48, LANES)] * 3...]
  transfers between devices with their start and end apart: 13 -> 13, of which waited for: 10 -> 8; matrix products, arithmetic and copies ran while one was open for 0% -> 0% of each run, Pallas kernels for 0% -> 0%
where the time goes in v2:
time: 59.8 us; the launch traced here: 59.4 us
  Pallas kernels  23.5 us (39%)
  starting transfers between devices  17.7 us (30%)
  waiting for transfers between devices  14.7 us (25%)
  between operations  2.13 us (4%)
  local copies, waits for them, and re-layouts  1.31 us (2%)
    pallas_call x1, Pallas kernels, per_device(): call(functools.partial(steps_kernel, rows), [shape(8 * rows, LANES)] * 2...  20.1 us
    ppermute x8, starting transfers between devices, swap(): return lax.ppermute(x, ('lon', 'lat'), pairs)  7.99 us
    ppermute x8, waiting for transfers between devices, swap(): return lax.ppermute(x, ('lon', 'lat'), pairs)  6.28 us
    ppermute x3, starting transfers between devices, send(): return lax.ppermute(x, ('lon', 'lat'), pairs)  5.1 us
    ppermute x1, waiting for transfers between devices, per_device(): lax.ppermute(packed, 'lon', [(i, (i + 1) % n_lon) for i in range(n_lon)])  4.75 us
    ppermute x1, starting transfers between devices, per_device(): lax.ppermute(packed, 'lon', [((i + 1) % n_lon, i) for i in range(n_lon)])  4.59 us
    ppermute x3, waiting for transfers between devices, send(): return lax.ppermute(x, ('lon', 'lat'), pairs)  3.7 us
    pallas_call x1, Pallas kernels, per_device(): call(functools.partial(edges_kernel, rows, cols), [shape(48, LANES)] * 3...  1.49 us
  transfers between devices with their start and end apart: 13, of which 8 were waited for; matrix products, arithmetic and copies ran while one was open for 0% of the time, Pallas kernels for 0%

profile of v2, /device:TPU:0, one launch (start us, length us, event | category | flops | bytes accessed | tf_op | source)
XLA Modules:
  0.0 59.4 jit_solution(4842840307207859896)
XLA Ops:
  0.6 0.0 copy-start.1
  0.6 1.5 %shard_map.146 = (f32[48,128]{1,0:T(8,128)S(1)}, f32[48,128]{1,0:T(8,128)S(1)}, f32[48,128]{1,0:T(8,128)S(1)}, s32[1]{0:T(128)}) custom-call(f32[128,128]{1,0:T(8,128)} %bitcast.12, f32[128,128]{1,0:T(8,128)} %bitcast.14, s32[16,128]{1,0:T(8,128)} %land.1, s32[16,128]{1,0:T(8,128)} %levels.1, s32[128]{0:T(128)} %partner_hbm.1), custom_call_target="tpu_custom_call" | custom-call | flops 1000000 | bytes 1000000 | tf_op jit(solution)/shard_map/pallas_call | solution.py:634
  2.1 0.0 copy-start
  2.8 0.0 copy-start.3
  2.8 0.0 copy-start.4
  2.9 8.8 %conditional.1 = (f32[48,128]{1,0:T(8,128)}, f32[48,128]{1,0:T(8,128)}, f32[48,128]{1,0:T(8,128)}) conditional(s32[]{:T(128)} %bitcast.3, (f32[48,128]{1,0:T(8,128)S(1)}, f32[48,128]{1,0:T(8,128)S(1)}, f32[48,128]{1,0:T(8,128)S(1)}) %tuple.40, (f32[48,128]{1,0:T(8,128)S(1)}, f32[48,128]{1,0:T(8,128)S(1)}, ...), branch_computations={%region_0.0_spmd, %region_1.0_spmd, %region_2.0_spmd, %region_3.0_... | conditional | bytes 295056 | solution.py:665
  2.9 3.0 %collective-permute-start.3 = (f32[48,128]{1,0:T(8,128)S(1)}, f32[48,128]{1,0:T(8,128)}, u32[]{:S(2)}, u32[]{:S(2)}) collective-permute-start(f32[48,128]{1,0:T(8,128)S(1)} %get-tuple-element.51), channel_id=1, source_target_pairs={{1,0},{2,1},{0,2},{5,4},{6,5},{4,6},{9,8},{10,9},{8,10},{13,12},{1... | collective-permute-start | bytes 73736 | tf_op jit(solution)/shard_map/cond/branch_1_fun/ppermute | solution.py:658
  5.9 1.9 %collective-permute-start.4 = (f32[48,128]{1,0:T(8,128)S(1)}, f32[48,128]{1,0:T(8,128)}, u32[]{:S(2)}, u32[]{:S(2)}) collective-permute-start(f32[48,128]{1,0:T(8,128)S(1)} %get-tuple-element.52), channel_id=1, source_target_pairs={{0,1},{1,2},{2,0},{4,5},{5,6},{6,4},{8,9},{9,10},{10,8},{12,13},{1... | collective-permute-start | bytes 73736 | tf_op jit(solution)/shard_map/cond/branch_1_fun/ppermute | solution.py:658
  7.8 0.2 collective-permute-start.5
  8.0 0.0 collective-permute-done.3
  8.0 3.7 %collective-permute-done.4 = f32[48,128]{1,0:T(8,128)} collective-permute-done((f32[48,128]{1,0:T(8,128)S(1)}, f32[48,128]{1,0:T(8,128)}, u32[]{:S(2)}, u32[]{:S(2)}) %collective-permute-start.4) | collective-permute-done | bytes 24608 | tf_op jit(solution)/shard_map/cond/branch_1_fun/ppermute | solution.py:658
  11.7 0.0 collective-permute-done.5
  11.7 0.0 copy-start.6
  11.7 0.0 copy-done.1
  11.7 0.0 copy-done
  11.7 0.0 copy-done.3
  11.7 0.0 copy-done.4
  11.7 0.6 %copy-done.6 = s32[128]{0:T(128)S(1)} copy-done((s32[128]{0:T(128)S(1)}, s32[128]{0:T(128)}, u32[]{:S(2)}) %copy-start.6) | copy-done | bytes 536
  12.3 0.0 copy-start.2
  12.3 1.0 %shard_map.147 = (f32[528,128]{1,0:T(8,128)S(1)}, f32[24,128]{1,0:T(8,128)S(1)}) custom-call(s32[1,128]{1,0:T(1,128)S(1)} %bitcast.16, f32[48,128]{1,0:T(8,128)} %get-tuple-element.101.first, f32[48,128]{1,0:T(8,128)} %get-tuple-element.102.second, f32[48,128]{1,0:T(8,128)} %get-tuple-element.103.third, f32[128,128]{1,0:T(8,128)S(1)} %bitcast.13, ...), custom_call_target="tpu_custom_call" | custom-call | flops 1000000 | bytes 1000000 | tf_op jit(solution)/shard_map/pallas_call | solution.py:674
  13.4 4.6 %collective-permute-start.25 = (f32[24,128]{1,0:T(8,128)S(1)}, f32[24,128]{1,0:T(8,128)S(1)}, u32[]{:S(2)}, u32[]{:S(2)}) collective-permute-start(f32[24,128]{1,0:T(8,128)S(1)} %get-tuple-element.105), channel_id=1, source_target_pairs={{4,0},{8,4},{12,8},{16,12},{20,16},{24,20},{28,24},{0,28},{5,1},{9... | collective-permute-start | bytes 36872 | tf_op jit(solution)/shard_map/ppermute | solution.py:706
  18.0 0.0 collective-permute-start.24
  18.6 0.0 copy-start.5
  18.6 0.0 copy-start.7
  18.6 0.0 copy-start.8
  18.6 0.0 copy-start.9
  18.7 0.0 copy-done.2
  18.7 0.6 %copy-done.5 = f32[6,128]{1,0:T(8,128)S(1)} copy-done((f32[6,128]{1,0:T(8,128)S(1)}, f32[6,128]{1,0:T(8,128)}, u32[]{:S(2)}) %copy-start.5) | copy-done | bytes 3096
  19.3 0.0 copy-done.7
  19.3 0.0 copy-done.8
  19.3 0.0 copy-done.9
  19.3 0.3 shard_map.148
  19.6 0.0 collective-permute-done.25.east_in
  19.6 4.7 %collective-permute-done.24.west_in = f32[24,128]{1,0:T(8,128)S(1)} collective-permute-done((f32[24,128]{1,0:T(8,128)S(1)}, f32[24,128]{1,0:T(8,128)S(1)}, u32[]{:S(2)}, u32[]{:S(2)}) %collective-permute-start.24) | collective-permute-done | bytes 12320 | tf_op jit(solution)/shard_map/ppermute | solution.py:705
  24.3 20.1 %shard_map.149 = (f32[128,128]{1,0:T(8,128)}, f32[128,128]{1,0:T(8,128)}, f32[72,128]{1,0:T(8,128)S(1)}, f32[72,128]{1,0:T(8,128)S(1)}) custom-call(f32[528,128]{1,0:T(8,128)S(1)} %get-tuple-element.104.ext, f32[24,128]{1,0:T(8,128)S(1)} %collective-permute-done.24.west_in, f32[24,128]{1,0:T(8,128)S(1)} %collective-permute-done.25.east_in, ...), custom_call_target="tpu_custom_call" | custom-call | flops 10000000000 | bytes 1000000 | tf_op jit(solution)/shard_map/pallas_call | solution.py:725
  44.4 0.0 collective-permute-start.26
  44.4 1.2 %collective-permute-done.26 = f32[72,128]{1,0:T(8,128)S(1)} collective-permute-done((f32[72,128]{1,0:T(8,128)S(1)}, f32[72,128]{1,0:T(8,128)S(1)}, u32[]{:S(2)}, u32[]{:S(2)}) %collective-permute-start.26) | collective-permute-done | bytes 36896 | tf_op jit(solution)/shard_map/ppermute | solution.py:736
  45.7 0.0 collective-permute-start.29
  45.7 1.1 %collective-permute-start.28 = (f32[72,128]{1,0:T(8,128)S(1)}, f32[72,128]{1,0:T(8,128)S(1)}, u32[]{:S(2)}, u32[]{:S(2)}) collective-permute-start(f32[72,128]{1,0:T(8,128)S(1)} %add.21), channel_id=1, source_target_pairs={{0,4},{1,5},{2,6},{3,7},{4,0},{5,1},{6,2},{7,3},{8,12},{9,13},{10,... | collective-permute-start | bytes 110600 | tf_op jit(solution)/shard_map/ppermute | solution.py:736
  46.7 2.4 %collective-permute-start.27 = (f32[72,128]{1,0:T(8,128)S(1)}, f32[72,128]{1,0:T(8,128)S(1)}, u32[]{:S(2)}, u32[]{:S(2)}) collective-permute-start(f32[72,128]{1,0:T(8,128)S(1)} %add.21), channel_id=1, source_target_pairs={{0,2},{1,3},{2,0},{3,1},{4,6},{5,7},{6,4},{7,5},{8,10},{9,11},{10,... | collective-permute-start | bytes 110600 | tf_op jit(solution)/shard_map/ppermute | solution.py:736
  49.1 1.4 %collective-permute-done.29 = f32[72,128]{1,0:T(8,128)S(1)} collective-permute-done((f32[72,128]{1,0:T(8,128)S(1)}, f32[72,128]{1,0:T(8,128)S(1)}, u32[]{:S(2)}, u32[]{:S(2)}) %collective-permute-start.29) | collective-permute-done | bytes 36896 | tf_op jit(solution)/shard_map/ppermute | solution.py:736
  50.5 0.0 collective-permute-done.28
  50.5 0.6 collective-permute-done.27
  51.1 0.1 collective-permute-start.32
  51.2 0.1 collective-permute-start.31
  51.3 4.3 %collective-permute-start.30 = (f32[72,128]{1,0:T(8,128)S(1)}, f32[72,128]{1,0:T(8,128)S(1)}, u32[]{:S(2)}, u32[]{:S(2)}) collective-permute-start(f32[72,128]{1,0:T(8,128)S(1)} %add_add_fusion.1), channel_id=1, source_target_pairs={{0,8},{1,9},{2,10},{3,11},{4,12},{5,13},{6,14},{7,15},{8,0},{9,1},... | collective-permute-start | bytes 110600 | tf_op jit(solution)/shard_map/ppermute | solution.py:736
  55.5 1.4 %collective-permute-done.32 = f32[72,128]{1,0:T(8,128)S(1)} collective-permute-done((f32[72,128]{1,0:T(8,128)S(1)}, f32[72,128]{1,0:T(8,128)S(1)}, u32[]{:S(2)}, u32[]{:S(2)}) %collective-permute-start.32) | collective-permute-done | bytes 36896 | tf_op jit(solution)/shard_map/ppermute | solution.py:736
  56.9 0.0 collective-permute-done.31
  56.9 0.6 collective-permute-done.30
  57.5 0.1 collective-permute-start.33
  57.6 1.2 %collective-permute-done.33.other = f32[72,128]{1,0:T(8,128)S(1)} collective-permute-done((f32[72,128]{1,0:T(8,128)S(1)}, f32[72,128]{1,0:T(8,128)S(1)}, u32[]{:S(2)}, u32[]{:S(2)}) %collective-permute-start.33) | collective-permute-done | bytes 36896 | tf_op jit(solution)/shard_map/ppermute | solution.py:736
  58.8 0.6 %shard_map.150 = (f32[6,128]{1,0:T(8,128)}, f32[128,128]{1,0:T(8,128)}, f32[1,128]{1,0:T(1,128)}) custom-call(f32[72,128]{1,0:T(8,128)S(1)} %add_add_fusion.mine, f32[72,128]{1,0:T(8,128)S(1)} %collective-permute-done.33.other), custom_call_target="tpu_custom_call" | custom-call | flops 1000000 | bytes 1000000 | tf_op jit(solution)/shard_map/pallas_call | solution.py:750
  (3 shorter events, 0.0 us)
Async XLA Ops:
  0.6 11.1 %copy-start.1 = (f32[2,4,16,128]{3,2,1,0:T(8,128)S(1)}, f32[2,4,16,128]{3,2,1,0:T(8,128)}, u32[]{:S(2)}) copy-start(f32[2,4,16,128]{3,2,1,0:T(8,128)} %param.23) | copy-start | bytes 196612
  2.1 9.6 %copy-start = (f32[2,4,16,128]{3,2,1,0:T(8,128)S(1)}, f32[2,4,16,128]{3,2,1,0:T(8,128)}, u32[]{:S(2)}) copy-start(f32[2,4,16,128]{3,2,1,0:T(8,128)} %param.19) | copy-start | bytes 196612
  2.8 8.9 %copy-start.3 = (s32[16,128]{1,0:T(8,128)S(1)}, s32[16,128]{1,0:T(8,128)}, u32[]{:S(2)}) copy-start(s32[16,128]{1,0:T(8,128)} %land.1) | copy-start | bytes 24580
  2.8 8.9 %copy-start.4 = (s32[16,128]{1,0:T(8,128)S(1)}, s32[16,128]{1,0:T(8,128)}, u32[]{:S(2)}) copy-start(s32[16,128]{1,0:T(8,128)} %levels.1) | copy-start | bytes 24580
  2.9 5.1 %collective-permute-start.3 = (f32[48,128]{1,0:T(8,128)S(1)}, f32[48,128]{1,0:T(8,128)}, u32[]{:S(2)}, u32[]{:S(2)}) collective-permute-start(f32[48,128]{1,0:T(8,128)S(1)} %get-tuple-element.51), channel_id=1, source_target_pairs={{1,0},{2,1},{0,2},{5,4},{6,5},{4,6},{9,8},{10,9},{8,10},{13,12},{1... | collective-permute-start | bytes 73736 | tf_op jit(solution)/shard_map/cond/branch_1_fun/ppermute | solution.py:658
  5.9 5.8 %collective-permute-start.4 = (f32[48,128]{1,0:T(8,128)S(1)}, f32[48,128]{1,0:T(8,128)}, u32[]{:S(2)}, u32[]{:S(2)}) collective-permute-start(f32[48,128]{1,0:T(8,128)S(1)} %get-tuple-element.52), channel_id=1, source_target_pairs={{0,1},{1,2},{2,0},{4,5},{5,6},{6,4},{8,9},{9,10},{10,8},{12,13},{1... | collective-permute-start | bytes 73736 | tf_op jit(solution)/shard_map/cond/branch_1_fun/ppermute | solution.py:658
  7.8 3.9 %collective-permute-start.5 = (f32[48,128]{1,0:T(8,128)S(1)}, f32[48,128]{1,0:T(8,128)}, u32[]{:S(2)}, u32[]{:S(2)}) collective-permute-start(f32[48,128]{1,0:T(8,128)S(1)} %get-tuple-element.53), channel_id=1, source_target_pairs={{0,1},{1,0},{2,3},{3,2},{4,5},{5,4},{6,7},{7,6},{8,9},{9,8},{10,11... | collective-permute-start | bytes 73736 | tf_op jit(solution)/shard_map/cond/branch_1_fun/ppermute | solution.py:658
  11.7 0.7 %copy-start.6 = (s32[128]{0:T(128)S(1)}, s32[128]{0:T(128)}, u32[]{:S(2)}) copy-start(s32[128]{0:T(128)} %partner_hbm.1) | copy-start | bytes 1540
  12.3 6.3 %copy-start.2 = (f32[128,128]{1,0:T(8,128)S(1)}, f32[128,128]{1,0:T(8,128)}, u32[]{:S(2)}) copy-start(f32[128,128]{1,0:T(8,128)} %w2.1) | copy-start | bytes 196612
  13.4 6.2 %collective-permute-start.25 = (f32[24,128]{1,0:T(8,128)S(1)}, f32[24,128]{1,0:T(8,128)S(1)}, u32[]{:S(2)}, u32[]{:S(2)}) collective-permute-start(f32[24,128]{1,0:T(8,128)S(1)} %get-tuple-element.105), channel_id=1, source_target_pairs={{4,0},{8,4},{12,8},{16,12},{20,16},{24,20},{28,24},{0,28},{5,1},{9... | collective-permute-start | bytes 36872 | tf_op jit(solution)/shard_map/ppermute | solution.py:706
  18.0 6.4 %collective-permute-start.24 = (f32[24,128]{1,0:T(8,128)S(1)}, f32[24,128]{1,0:T(8,128)S(1)}, u32[]{:S(2)}, u32[]{:S(2)}) collective-permute-start(f32[24,128]{1,0:T(8,128)S(1)} %get-tuple-element.105), channel_id=1, source_target_pairs={{0,4},{4,8},{8,12},{12,16},{16,20},{20,24},{24,28},{28,0},{1,5},{5... | collective-permute-start | bytes 36872 | tf_op jit(solution)/shard_map/ppermute | solution.py:705
  18.6 0.7 %copy-start.5 = (f32[6,128]{1,0:T(8,128)S(1)}, f32[6,128]{1,0:T(8,128)}, u32[]{:S(2)}) copy-start(f32[6,128]{1,0:T(8,128)} %w1.1) | copy-start | bytes 9220
  18.6 0.7 %copy-start.7 = (f32[128]{0:T(128)S(1)}, f32[128]{0:T(128)}, u32[]{:S(2)}) copy-start(f32[128]{0:T(128)} %param.25) | copy-start | bytes 1540
  18.6 0.7 %copy-start.8 = (f32[128]{0:T(128)S(1)}, f32[128]{0:T(128)}, u32[]{:S(2)}) copy-start(f32[128]{0:T(128)} %param.27) | copy-start | bytes 1540
  18.6 0.7 %copy-start.9 = (f32[128]{0:T(128)S(1)}, f32[128]{0:T(128)}, u32[]{:S(2)}) copy-start(f32[128]{0:T(128)} %param.28) | copy-start | bytes 1540
  44.4 1.2 %collective-permute-start.26 = (f32[72,128]{1,0:T(8,128)S(1)}, f32[72,128]{1,0:T(8,128)S(1)}, u32[]{:S(2)}, u32[]{:S(2)}) collective-permute-start(f32[72,128]{1,0:T(8,128)S(1)} %get-tuple-element.113), channel_id=1, source_target_pairs={{0,1},{1,0},{2,3},{3,2},{4,5},{5,4},{6,7},{7,6},{8,9},{9,8},{10,11... | collective-permute-start | bytes 110600 | tf_op jit(solution)/shard_map/ppermute | solution.py:736
  45.7 4.9 %collective-permute-start.29 = (f32[72,128]{1,0:T(8,128)S(1)}, f32[72,128]{1,0:T(8,128)S(1)}, u32[]{:S(2)}, u32[]{:S(2)}) collective-permute-start(f32[72,128]{1,0:T(8,128)S(1)} %add.21), channel_id=1, source_target_pairs={{0,6},{1,7},{2,4},{3,5},{4,2},{5,3},{6,0},{7,1},{8,14},{9,15},{10,... | collective-permute-start | bytes 110600 | tf_op jit(solution)/shard_map/ppermute | solution.py:736
  45.7 4.9 %collective-permute-start.28 = (f32[72,128]{1,0:T(8,128)S(1)}, f32[72,128]{1,0:T(8,128)S(1)}, u32[]{:S(2)}, u32[]{:S(2)}) collective-permute-start(f32[72,128]{1,0:T(8,128)S(1)} %add.21), channel_id=1, source_target_pairs={{0,4},{1,5},{2,6},{3,7},{4,0},{5,1},{6,2},{7,3},{8,12},{9,13},{10,... | collective-permute-start | bytes 110600 | tf_op jit(solution)/shard_map/ppermute | solution.py:736
  46.7 4.4 %collective-permute-start.27 = (f32[72,128]{1,0:T(8,128)S(1)}, f32[72,128]{1,0:T(8,128)S(1)}, u32[]{:S(2)}, u32[]{:S(2)}) collective-permute-start(f32[72,128]{1,0:T(8,128)S(1)} %add.21), channel_id=1, source_target_pairs={{0,2},{1,3},{2,0},{3,1},{4,6},{5,7},{6,4},{7,5},{8,10},{9,11},{10,... | collective-permute-start | bytes 110600 | tf_op jit(solution)/shard_map/ppermute | solution.py:736
  51.1 5.8 %collective-permute-start.32 = (f32[72,128]{1,0:T(8,128)S(1)}, f32[72,128]{1,0:T(8,128)S(1)}, u32[]{:S(2)}, u32[]{:S(2)}) collective-permute-start(f32[72,128]{1,0:T(8,128)S(1)} %add_add_fusion.1), channel_id=1, source_target_pairs={{0,24},{1,25},{2,26},{3,27},{4,28},{5,29},{6,30},{7,31},{8,16},{9,... | collective-permute-start | bytes 110600 | tf_op jit(solution)/shard_map/ppermute | solution.py:736
  51.2 5.7 %collective-permute-start.31 = (f32[72,128]{1,0:T(8,128)S(1)}, f32[72,128]{1,0:T(8,128)S(1)}, u32[]{:S(2)}, u32[]{:S(2)}) collective-permute-start(f32[72,128]{1,0:T(8,128)S(1)} %add_add_fusion.1), channel_id=1, source_target_pairs={{0,16},{1,17},{2,18},{3,19},{4,20},{5,21},{6,22},{7,23},{8,24},{9,... | collective-permute-start | bytes 110600 | tf_op jit(solution)/shard_map/ppermute | solution.py:736
  51.3 6.2 %collective-permute-start.30 = (f32[72,128]{1,0:T(8,128)S(1)}, f32[72,128]{1,0:T(8,128)S(1)}, u32[]{:S(2)}, u32[]{:S(2)}) collective-permute-start(f32[72,128]{1,0:T(8,128)S(1)} %add_add_fusion.1), channel_id=1, source_target_pairs={{0,8},{1,9},{2,10},{3,11},{4,12},{5,13},{6,14},{7,15},{8,0},{9,1},... | collective-permute-start | bytes 110600 | tf_op jit(solution)/shard_map/ppermute | solution.py:736
  57.5 1.3 %collective-permute-start.33 = (f32[72,128]{1,0:T(8,128)S(1)}, f32[72,128]{1,0:T(8,128)S(1)}, u32[]{:S(2)}, u32[]{:S(2)}) collective-permute-start(f32[72,128]{1,0:T(8,128)S(1)} %add_add_fusion.mine), channel_id=1, source_target_pairs={{0,1},{1,0},{2,3},{3,2},{4,5},{5,4},{6,7},{7,6},{8,9},{9,8},{10,11... | collective-permute-start | bytes 110600 | tf_op jit(solution)/shard_map/ppermute | solution.py:736

commit v3 on v2

--- a/solution.py
+++ b/solution.py
@@ -13,6 +13,7 @@
 HID = 128
 LANES = 128
 HALO = 3
+GROUP = 8
 SLOT = 2 * HALO
 F32 = jnp.float32
 BF16 = jnp.bfloat16
@@ -40,6 +41,7 @@
     north,
     south_last,
     turn_out,
+    source_out,
     tracer,
     cot,
     land,
@@ -63,6 +65,9 @@
     for copy in copies:
         copy.wait()
     turn_out[0] = lax.rem(lax.div(partner[0], cols) + lax.axis_index("lon"), lax.axis_size("lon"))
+
+    lane = iota((8, LANES), 1)
+    source_out[...] = jnp.bitwise_and(partner[0] - lane, LANES - 1)
 
     at_top = lax.axis_index("lat") == lax.axis_size("lat") - 1
     depth = (land[...] * levels[...]).astype(F32)
@@ -113,14 +118,14 @@
 
 
 def assemble_kernel(
-    rows, partner, first, second, third, tracer, cot, land, levels, ext, packed
+    rows, source_in, first, second, third, tracer, cot, land, levels, ext, packed
 ):
     lane = iota((8, LANES), 1)
     lat, n_lat = lax.axis_index("lat"), lax.axis_size("lat")
     at_top = lat == n_lat - 1
     below_top = lat == n_lat - 2
     at_bottom = lat == 0
-    source = jnp.broadcast_to(jnp.bitwise_and(partner[...], LANES - 1), (8, LANES))
+    source = source_in[...]
     offset = jnp.broadcast_to(source[:, 0:1], (8, LANES))
 
     def mirrored(place):
@@ -349,7 +354,10 @@
                     slope[tile] = kappa * (1.0 - part)
             return carry
 
-        lax.fori_loop(0, steps, body, 0)
+        if steps == 1:
+            body(0, 0)
+        else:
+            lax.fori_loop(0, steps, body, 0)
 
     def edge_masks(i):
         east_w = east(*wet[i])
@@ -497,13 +505,16 @@
                     bar_tiles[tile] = cells[:, lanes] - v + pltpu.roll(v, 1, 0)
             return carry
 
-        lax.fori_loop(0, steps, body, 0)
+        if steps == 1:
+            body(0, 0)
+        else:
+            lax.fori_loop(0, steps, body, 0)
 
     low, high = HALO, rows + HALO - 1
     step0 = (c_tiles0, slope0, x0, h1b0, h1f0, h2f0)
     own = rows // 2
-    closure(0, own // 4, 4, True, *step0)
-    closure(own, (n_tiles // 2 - own) // 2, 2, False, *step0)
+    closure(0, own // GROUP, GROUP, True, *step0)
+    closure(own, 1, n_tiles // 2 - own, False, *step0)
     kappa0 = kappas(0, total - 1)
     ce0, cn0 = coefficients(kappa0, low - 2, high + 2)
     de0, dn0 = diffs(c0, low - 2, high + 2)
@@ -515,7 +526,7 @@
     for tile in range(tiles1, n_tiles):
         c_tiles1[tile] = zero
     step1 = (c_tiles1, slope1, x1, h1b1, h1f1, h2f1)
-    closure(0, own // 4, 4, True, *step1)
+    closure(0, own // GROUP, GROUP, True, *step1)
     closure(own, 1, 2, True, *step1)
     closure(own + 2, 1, 1, False, *step1)
     kappa1 = kappas(low - 2, high + 2)
@@ -537,7 +548,7 @@
     acc_w2[...] = jnp.zeros_like(acc_w2)
     acc_a1[...] = jnp.zeros_like(acc_a1)
     acc_head[...] = jnp.zeros_like(acc_head)
-    closure_back(0, own // 4, 4, True, *step1[1:])
+    closure_back(0, own // GROUP, GROUP, True, *step1[1:])
     closure_back(own, 1, 2, False, *step1[1:])
     side_bar = bar_tiles[side_tile]
     lam1 = {}
@@ -550,7 +561,7 @@
     bars = kappa_bars(de0, dn0, le, ln, low, high)
     for i in range(low, high + 1):
         d3_tiles[tile_of[i]] = bars[i][0]
-    closure_back(0, own // 4, 4, True, *step0[1:])
+    closure_back(0, own // GROUP, GROUP, True, *step0[1:])
     for i in range(low, high + 1):
         out_grad[pl.ds(i - low, 8, stride=rows), :] = direct[i][0] + bar_tiles[tile_of[i]]
     first = [None] * 6
@@ -631,11 +642,11 @@
     cot2 = cotangent.reshape(8 * rows, cols)
 
     args = (tracer2, cot2, land_mask, level_counts, fold_partner)
-    south_first, north, south_last, turn = call(
+    south_first, north, south_last, turn, source = call(
         functools.partial(edges_kernel, rows, cols),
-        [shape(48, LANES)] * 3 + [shape(1, dtype=jnp.int32)],
+        [shape(48, LANES)] * 3 + [shape(1, dtype=jnp.int32), shape(8, LANES, dtype=jnp.int32)],
         [HBM] * len(args),
-        out_specs=[VMEM] * 3 + [SMEM],
+        out_specs=[VMEM] * 3 + [SMEM, VMEM],
         scratch=[pltpu.VMEM(x.shape, x.dtype) for x in args[:4]]
         + [pltpu.SMEM(fold_partner.shape, fold_partner.dtype)]
         + [pltpu.SemaphoreType.DMA((len(args),))],
@@ -676,7 +687,7 @@
         [shape(24 * total, LANES), shape(24, LANES)],
         [VMEM] * 8,
     )(
-        fold_partner.reshape(1, cols),
+        source,
         from_first,
         from_second,
         from_third,

time: 59.8 us -> 58 us (0.970)
  Pallas kernels: 23.5 us -> 21.7 us
    pallas_call x1, Pallas kernels: 20.1 us -> 18.2 us  [per_device(): call(functools.partial(steps_kernel, rows), [shape(8 * rows, LANES)] * 2...]
where the time goes in v3:
time: 58 us; the launch traced here: 57.6 us
  Pallas kernels  21.7 us (37%)
  starting transfers between devices  17.7 us (31%)
  waiting for transfers between devices  14.7 us (25%)
  between operations  2.13 us (4%)
  local copies, waits for them, and re-layouts  1.37 us (2%)
    pallas_call x1, Pallas kernels, per_device(): call(functools.partial(steps_kernel, rows), [shape(8 * rows, LANES)] * 2...  18.2 us
    ppermute x8, starting transfers between devices, swap(): return lax.ppermute(x, ('lon', 'lat'), pairs)  7.99 us
    ppermute x8, waiting for transfers between devices, swap(): return lax.ppermute(x, ('lon', 'lat'), pairs)  6.28 us
    ppermute x3, starting transfers between devices, send(): return lax.ppermute(x, ('lon', 'lat'), pairs)  5.1 us
    ppermute x1, waiting for transfers between devices, per_device(): lax.ppermute(packed, 'lon', [(i, (i + 1) % n_lon) for i in range(n_lon)])  4.75 us
    ppermute x1, starting transfers between devices, per_device(): lax.ppermute(packed, 'lon', [((i + 1) % n_lon, i) for i in range(n_lon)])  4.59 us
    ppermute x3, waiting for transfers between devices, send(): return lax.ppermute(x, ('lon', 'lat'), pairs)  3.7 us
    pallas_call x1, Pallas kernels, per_device(): call(functools.partial(edges_kernel, rows, cols), [shape(48, LANES)] * 3...  1.56 us
  transfers between devices with their start and end apart: 13, of which 8 were waited for; matrix products, arithmetic and copies ran while one was open for 0% of the time, Pallas kernels for 0%

profile of v3, /device:TPU:0, one launch (start us, length us, event | category | flops | bytes accessed | tf_op | source)
XLA Modules:
  0.0 57.6 jit_solution(8532218840814388041)
XLA Ops:
  0.6 0.0 copy-start.1
  0.6 1.6 %shard_map.146 = (f32[48,128]{1,0:T(8,128)S(1)}, f32[48,128]{1,0:T(8,128)S(1)}, f32[48,128]{1,0:T(8,128)S(1)}, s32[1]{0:T(128)}, s32[8,128]{1,0:T(8,128)}) custom-call(f32[128,128]{1,0:T(8,128)} %bitcast.11, f32[128,128]{1,0:T(8,128)} %bitcast.13, s32[16,128]{1,0:T(8,128)} %land.1, s32[16,128]{1,0:T(8,128)} %levels.1, s32[128]{0:T(128)} %partner_hbm.1), custom_call_target="tpu_custom_call" | custom-call | flops 1000000 | bytes 1000000 | tf_op jit(solution)/shard_map/pallas_call | solution.py:645
  2.2 0.0 copy-start
  2.9 0.0 copy-start.3
  2.9 0.0 copy-start.4
  2.9 8.8 %conditional.1 = (f32[48,128]{1,0:T(8,128)}, f32[48,128]{1,0:T(8,128)}, f32[48,128]{1,0:T(8,128)}) conditional(s32[]{:T(128)} %bitcast.2, (f32[48,128]{1,0:T(8,128)S(1)}, f32[48,128]{1,0:T(8,128)S(1)}, f32[48,128]{1,0:T(8,128)S(1)}) %tuple.40, (f32[48,128]{1,0:T(8,128)S(1)}, f32[48,128]{1,0:T(8,128)S(1)}, ...), branch_computations={%region_0.0_spmd, %region_1.0_spmd, %region_2.0_spmd, %region_3.0_... | conditional | bytes 295056 | solution.py:676
  3.0 3.0 %collective-permute-start.21 = (f32[48,128]{1,0:T(8,128)S(1)}, f32[48,128]{1,0:T(8,128)}, u32[]{:S(2)}, u32[]{:S(2)}) collective-permute-start(f32[48,128]{1,0:T(8,128)S(1)} %get-tuple-element.69), channel_id=1, source_target_pairs={{1,0},{2,1},{0,2},{5,4},{6,5},{4,6},{9,8},{10,9},{8,10},{13,12},{1... | collective-permute-start | bytes 73736 | tf_op jit(solution)/shard_map/cond/branch_7_fun/ppermute | solution.py:669
  6.0 1.9 %collective-permute-start.22 = (f32[48,128]{1,0:T(8,128)S(1)}, f32[48,128]{1,0:T(8,128)}, u32[]{:S(2)}, u32[]{:S(2)}) collective-permute-start(f32[48,128]{1,0:T(8,128)S(1)} %get-tuple-element.70), channel_id=1, source_target_pairs={{0,1},{1,2},{2,0},{4,5},{5,6},{6,4},{8,9},{9,10},{10,8},{12,13},{1... | collective-permute-start | bytes 73736 | tf_op jit(solution)/shard_map/cond/branch_7_fun/ppermute | solution.py:669
  7.9 0.2 collective-permute-start.23
  8.1 0.0 collective-permute-done.21
  8.1 3.7 %collective-permute-done.22 = f32[48,128]{1,0:T(8,128)} collective-permute-done((f32[48,128]{1,0:T(8,128)S(1)}, f32[48,128]{1,0:T(8,128)}, u32[]{:S(2)}, u32[]{:S(2)}) %collective-permute-start.22) | collective-permute-done | bytes 24608 | tf_op jit(solution)/shard_map/cond/branch_7_fun/ppermute | solution.py:669
  11.8 0.0 collective-permute-done.23
  11.8 0.0 copy-done.1
  11.8 0.0 copy-done
  11.8 0.0 copy-done.3
  11.8 0.0 copy-done.4
  11.8 0.0 copy-start.5
  11.8 0.7 %copy-done.5 = s32[8,128]{1,0:T(8,128)S(1)} copy-done((s32[8,128]{1,0:T(8,128)S(1)}, s32[8,128]{1,0:T(8,128)}, u32[]{:S(2)}) %copy-start.5) | copy-done | bytes 4120
  12.5 0.0 copy-start.2
  12.5 1.0 %shard_map.147 = (f32[528,128]{1,0:T(8,128)S(1)}, f32[24,128]{1,0:T(8,128)S(1)}) custom-call(s32[8,128]{1,0:T(8,128)S(1)} %copy-done.5, f32[48,128]{1,0:T(8,128)} %get-tuple-element.103.first, f32[48,128]{1,0:T(8,128)} %get-tuple-element.104.second, f32[48,128]{1,0:T(8,128)} %get-tuple-element.105.third, f32[128,128]{1,0:T(8,128)S(1)} %bitcast.12, ...), custom_call_target="tpu_custom_call" | custom-call | flops 1000000 | bytes 1000000 | tf_op jit(solution)/shard_map/pallas_call | solution.py:685
  13.5 4.6 %collective-permute-start.25 = (f32[24,128]{1,0:T(8,128)S(1)}, f32[24,128]{1,0:T(8,128)S(1)}, u32[]{:S(2)}, u32[]{:S(2)}) collective-permute-start(f32[24,128]{1,0:T(8,128)S(1)} %get-tuple-element.107), channel_id=1, source_target_pairs={{4,0},{8,4},{12,8},{16,12},{20,16},{24,20},{28,24},{0,28},{5,1},{9... | collective-permute-start | bytes 36872 | tf_op jit(solution)/shard_map/ppermute | solution.py:717
  18.1 0.0 collective-permute-start.24
  18.8 0.0 copy-start.6
  18.8 0.0 copy-start.7
  18.8 0.0 copy-start.8
  18.8 0.0 copy-start.9
  18.8 0.0 copy-done.2
  18.8 0.6 %copy-done.6 = f32[6,128]{1,0:T(8,128)S(1)} copy-done((f32[6,128]{1,0:T(8,128)S(1)}, f32[6,128]{1,0:T(8,128)}, u32[]{:S(2)}) %copy-start.6) | copy-done | bytes 3096
  19.4 0.0 copy-done.7
  19.4 0.0 copy-done.8
  19.4 0.0 copy-done.9
  19.5 0.3 shard_map.148
  19.7 0.0 collective-permute-done.25.east_in
  19.7 4.7 %collective-permute-done.24.west_in = f32[24,128]{1,0:T(8,128)S(1)} collective-permute-done((f32[24,128]{1,0:T(8,128)S(1)}, f32[24,128]{1,0:T(8,128)S(1)}, u32[]{:S(2)}, u32[]{:S(2)}) %collective-permute-start.24) | collective-permute-done | bytes 12320 | tf_op jit(solution)/shard_map/ppermute | solution.py:716
  24.5 18.2 %shard_map.149 = (f32[128,128]{1,0:T(8,128)}, f32[128,128]{1,0:T(8,128)}, f32[72,128]{1,0:T(8,128)S(1)}, f32[72,128]{1,0:T(8,128)S(1)}) custom-call(f32[528,128]{1,0:T(8,128)S(1)} %get-tuple-element.106.ext, f32[24,128]{1,0:T(8,128)S(1)} %collective-permute-done.24.west_in, f32[24,128]{1,0:T(8,128)S(1)} %collective-permute-done.25.east_in, ...), custom_call_target="tpu_custom_call" | custom-call | flops 10000000000 | bytes 1000000 | tf_op jit(solution)/shard_map/pallas_call | solution.py:736
  42.7 0.0 collective-permute-start.26
  42.7 1.2 %collective-permute-done.26 = f32[72,128]{1,0:T(8,128)S(1)} collective-permute-done((f32[72,128]{1,0:T(8,128)S(1)}, f32[72,128]{1,0:T(8,128)S(1)}, u32[]{:S(2)}, u32[]{:S(2)}) %collective-permute-start.26) | collective-permute-done | bytes 36896 | tf_op jit(solution)/shard_map/ppermute | solution.py:747
  43.9 0.0 collective-permute-start.29
  43.9 1.1 %collective-permute-start.28 = (f32[72,128]{1,0:T(8,128)S(1)}, f32[72,128]{1,0:T(8,128)S(1)}, u32[]{:S(2)}, u32[]{:S(2)}) collective-permute-start(f32[72,128]{1,0:T(8,128)S(1)} %add.21), channel_id=1, source_target_pairs={{0,4},{1,5},{2,6},{3,7},{4,0},{5,1},{6,2},{7,3},{8,12},{9,13},{10,... | collective-permute-start | bytes 110600 | tf_op jit(solution)/shard_map/ppermute | solution.py:747
  45.0 2.4 %collective-permute-start.27 = (f32[72,128]{1,0:T(8,128)S(1)}, f32[72,128]{1,0:T(8,128)S(1)}, u32[]{:S(2)}, u32[]{:S(2)}) collective-permute-start(f32[72,128]{1,0:T(8,128)S(1)} %add.21), channel_id=1, source_target_pairs={{0,2},{1,3},{2,0},{3,1},{4,6},{5,7},{6,4},{7,5},{8,10},{9,11},{10,... | collective-permute-start | bytes 110600 | tf_op jit(solution)/shard_map/ppermute | solution.py:747
  47.4 1.4 %collective-permute-done.29 = f32[72,128]{1,0:T(8,128)S(1)} collective-permute-done((f32[72,128]{1,0:T(8,128)S(1)}, f32[72,128]{1,0:T(8,128)S(1)}, u32[]{:S(2)}, u32[]{:S(2)}) %collective-permute-start.29) | collective-permute-done | bytes 36896 | tf_op jit(solution)/shard_map/ppermute | solution.py:747
  48.7 0.0 collective-permute-done.28
  48.7 0.6 collective-permute-done.27
  49.3 0.1 collective-permute-start.32
  49.4 0.1 collective-permute-start.31
  49.5 4.3 %collective-permute-start.30 = (f32[72,128]{1,0:T(8,128)S(1)}, f32[72,128]{1,0:T(8,128)S(1)}, u32[]{:S(2)}, u32[]{:S(2)}) collective-permute-start(f32[72,128]{1,0:T(8,128)S(1)} %add_add_fusion.1), channel_id=1, source_target_pairs={{0,8},{1,9},{2,10},{3,11},{4,12},{5,13},{6,14},{7,15},{8,0},{9,1},... | collective-permute-start | bytes 110600 | tf_op jit(solution)/shard_map/ppermute | solution.py:747
  53.8 1.4 %collective-permute-done.32 = f32[72,128]{1,0:T(8,128)S(1)} collective-permute-done((f32[72,128]{1,0:T(8,128)S(1)}, f32[72,128]{1,0:T(8,128)S(1)}, u32[]{:S(2)}, u32[]{:S(2)}) %collective-permute-start.32) | collective-permute-done | bytes 36896 | tf_op jit(solution)/shard_map/ppermute | solution.py:747
  55.1 0.0 collective-permute-done.31
  55.1 0.6 collective-permute-done.30
  55.7 0.1 collective-permute-start.33
  55.8 1.2 %collective-permute-done.33.other = f32[72,128]{1,0:T(8,128)S(1)} collective-permute-done((f32[72,128]{1,0:T(8,128)S(1)}, f32[72,128]{1,0:T(8,128)S(1)}, u32[]{:S(2)}, u32[]{:S(2)}) %collective-permute-start.33) | collective-permute-done | bytes 36896 | tf_op jit(solution)/shard_map/ppermute | solution.py:747
  57.0 0.6 %shard_map.150 = (f32[6,128]{1,0:T(8,128)}, f32[128,128]{1,0:T(8,128)}, f32[1,128]{1,0:T(1,128)}) custom-call(f32[72,128]{1,0:T(8,128)S(1)} %add_add_fusion.mine, f32[72,128]{1,0:T(8,128)S(1)} %collective-permute-done.33.other), custom_call_target="tpu_custom_call" | custom-call | flops 1000000 | bytes 1000000 | tf_op jit(solution)/shard_map/pallas_call | solution.py:761
  (3 shorter events, 0.0 us)
Async XLA Ops:
  0.6 11.1 %copy-start.1 = (f32[2,4,16,128]{3,2,1,0:T(8,128)S(1)}, f32[2,4,16,128]{3,2,1,0:T(8,128)}, u32[]{:S(2)}) copy-start(f32[2,4,16,128]{3,2,1,0:T(8,128)} %param.23) | copy-start | bytes 196612
  2.2 9.6 %copy-start = (f32[2,4,16,128]{3,2,1,0:T(8,128)S(1)}, f32[2,4,16,128]{3,2,1,0:T(8,128)}, u32[]{:S(2)}) copy-start(f32[2,4,16,128]{3,2,1,0:T(8,128)} %param.19) | copy-start | bytes 196612
  2.9 8.9 %copy-start.3 = (s32[16,128]{1,0:T(8,128)S(1)}, s32[16,128]{1,0:T(8,128)}, u32[]{:S(2)}) copy-start(s32[16,128]{1,0:T(8,128)} %land.1) | copy-start | bytes 24580
  2.9 8.9 %copy-start.4 = (s32[16,128]{1,0:T(8,128)S(1)}, s32[16,128]{1,0:T(8,128)}, u32[]{:S(2)}) copy-start(s32[16,128]{1,0:T(8,128)} %levels.1) | copy-start | bytes 24580
  3.0 5.1 %collective-permute-start.21 = (f32[48,128]{1,0:T(8,128)S(1)}, f32[48,128]{1,0:T(8,128)}, u32[]{:S(2)}, u32[]{:S(2)}) collective-permute-start(f32[48,128]{1,0:T(8,128)S(1)} %get-tuple-element.69), channel_id=1, source_target_pairs={{1,0},{2,1},{0,2},{5,4},{6,5},{4,6},{9,8},{10,9},{8,10},{13,12},{1... | collective-permute-start | bytes 73736 | tf_op jit(solution)/shard_map/cond/branch_7_fun/ppermute | solution.py:669
  6.0 5.8 %collective-permute-start.22 = (f32[48,128]{1,0:T(8,128)S(1)}, f32[48,128]{1,0:T(8,128)}, u32[]{:S(2)}, u32[]{:S(2)}) collective-permute-start(f32[48,128]{1,0:T(8,128)S(1)} %get-tuple-element.70), channel_id=1, source_target_pairs={{0,1},{1,2},{2,0},{4,5},{5,6},{6,4},{8,9},{9,10},{10,8},{12,13},{1... | collective-permute-start | bytes 73736 | tf_op jit(solution)/shard_map/cond/branch_7_fun/ppermute | solution.py:669
  7.9 3.9 %collective-permute-start.23 = (f32[48,128]{1,0:T(8,128)S(1)}, f32[48,128]{1,0:T(8,128)}, u32[]{:S(2)}, u32[]{:S(2)}) collective-permute-start(f32[48,128]{1,0:T(8,128)S(1)} %get-tuple-element.71), channel_id=1, source_target_pairs={{0,1},{1,0},{2,3},{3,2},{4,5},{5,4},{6,7},{7,6},{8,9},{9,8},{10,11... | collective-permute-start | bytes 73736 | tf_op jit(solution)/shard_map/cond/branch_7_fun/ppermute | solution.py:669
  11.8 0.7 %copy-start.5 = (s32[8,128]{1,0:T(8,128)S(1)}, s32[8,128]{1,0:T(8,128)}, u32[]{:S(2)}) copy-start(s32[8,128]{1,0:T(8,128)} %get-tuple-element.98.source_in) | copy-start | bytes 12292
  12.5 6.3 %copy-start.2 = (f32[128,128]{1,0:T(8,128)S(1)}, f32[128,128]{1,0:T(8,128)}, u32[]{:S(2)}) copy-start(f32[128,128]{1,0:T(8,128)} %w2.1) | copy-start | bytes 196612
  13.5 6.2 %collective-permute-start.25 = (f32[24,128]{1,0:T(8,128)S(1)}, f32[24,128]{1,0:T(8,128)S(1)}, u32[]{:S(2)}, u32[]{:S(2)}) collective-permute-start(f32[24,128]{1,0:T(8,128)S(1)} %get-tuple-element.107), channel_id=1, source_target_pairs={{4,0},{8,4},{12,8},{16,12},{20,16},{24,20},{28,24},{0,28},{5,1},{9... | collective-permute-start | bytes 36872 | tf_op jit(solution)/shard_map/ppermute | solution.py:717
  18.1 6.4 %collective-permute-start.24 = (f32[24,128]{1,0:T(8,128)S(1)}, f32[24,128]{1,0:T(8,128)S(1)}, u32[]{:S(2)}, u32[]{:S(2)}) collective-permute-start(f32[24,128]{1,0:T(8,128)S(1)} %get-tuple-element.107), channel_id=1, source_target_pairs={{0,4},{4,8},{8,12},{12,16},{16,20},{20,24},{24,28},{28,0},{1,5},{5... | collective-permute-start | bytes 36872 | tf_op jit(solution)/shard_map/ppermute | solution.py:716
  18.8 0.7 %copy-start.6 = (f32[6,128]{1,0:T(8,128)S(1)}, f32[6,128]{1,0:T(8,128)}, u32[]{:S(2)}) copy-start(f32[6,128]{1,0:T(8,128)} %w1.1) | copy-start | bytes 9220
  18.8 0.7 %copy-start.7 = (f32[128]{0:T(128)S(1)}, f32[128]{0:T(128)}, u32[]{:S(2)}) copy-start(f32[128]{0:T(128)} %param.25) | copy-start | bytes 1540
  18.8 0.7 %copy-start.8 = (f32[128]{0:T(128)S(1)}, f32[128]{0:T(128)}, u32[]{:S(2)}) copy-start(f32[128]{0:T(128)} %param.27) | copy-start | bytes 1540
  18.8 0.7 %copy-start.9 = (f32[128]{0:T(128)S(1)}, f32[128]{0:T(128)}, u32[]{:S(2)}) copy-start(f32[128]{0:T(128)} %param.28) | copy-start | bytes 1540
  42.7 1.2 %collective-permute-start.26 = (f32[72,128]{1,0:T(8,128)S(1)}, f32[72,128]{1,0:T(8,128)S(1)}, u32[]{:S(2)}, u32[]{:S(2)}) collective-permute-start(f32[72,128]{1,0:T(8,128)S(1)} %get-tuple-element.115), channel_id=1, source_target_pairs={{0,1},{1,0},{2,3},{3,2},{4,5},{5,4},{6,7},{7,6},{8,9},{9,8},{10,11... | collective-permute-start | bytes 110600 | tf_op jit(solution)/shard_map/ppermute | solution.py:747
  43.9 4.9 %collective-permute-start.29 = (f32[72,128]{1,0:T(8,128)S(1)}, f32[72,128]{1,0:T(8,128)S(1)}, u32[]{:S(2)}, u32[]{:S(2)}) collective-permute-start(f32[72,128]{1,0:T(8,128)S(1)} %add.21), channel_id=1, source_target_pairs={{0,6},{1,7},{2,4},{3,5},{4,2},{5,3},{6,0},{7,1},{8,14},{9,15},{10,... | collective-permute-start | bytes 110600 | tf_op jit(solution)/shard_map/ppermute | solution.py:747
  43.9 4.9 %collective-permute-start.28 = (f32[72,128]{1,0:T(8,128)S(1)}, f32[72,128]{1,0:T(8,128)S(1)}, u32[]{:S(2)}, u32[]{:S(2)}) collective-permute-start(f32[72,128]{1,0:T(8,128)S(1)} %add.21), channel_id=1, source_target_pairs={{0,4},{1,5},{2,6},{3,7},{4,0},{5,1},{6,2},{7,3},{8,12},{9,13},{10,... | collective-permute-start | bytes 110600 | tf_op jit(solution)/shard_map/ppermute | solution.py:747
  45.0 4.4 %collective-permute-start.27 = (f32[72,128]{1,0:T(8,128)S(1)}, f32[72,128]{1,0:T(8,128)S(1)}, u32[]{:S(2)}, u32[]{:S(2)}) collective-permute-start(f32[72,128]{1,0:T(8,128)S(1)} %add.21), channel_id=1, source_target_pairs={{0,2},{1,3},{2,0},{3,1},{4,6},{5,7},{6,4},{7,5},{8,10},{9,11},{10,... | collective-permute-start | bytes 110600 | tf_op jit(solution)/shard_map/ppermute | solution.py:747
  49.3 5.8 %collective-permute-start.32 = (f32[72,128]{1,0:T(8,128)S(1)}, f32[72,128]{1,0:T(8,128)S(1)}, u32[]{:S(2)}, u32[]{:S(2)}) collective-permute-start(f32[72,128]{1,0:T(8,128)S(1)} %add_add_fusion.1), channel_id=1, source_target_pairs={{0,24},{1,25},{2,26},{3,27},{4,28},{5,29},{6,30},{7,31},{8,16},{9,... | collective-permute-start | bytes 110600 | tf_op jit(solution)/shard_map/ppermute | solution.py:747
  49.4 5.7 %collective-permute-start.31 = (f32[72,128]{1,0:T(8,128)S(1)}, f32[72,128]{1,0:T(8,128)S(1)}, u32[]{:S(2)}, u32[]{:S(2)}) collective-permute-start(f32[72,128]{1,0:T(8,128)S(1)} %add_add_fusion.1), channel_id=1, source_target_pairs={{0,16},{1,17},{2,18},{3,19},{4,20},{5,21},{6,22},{7,23},{8,24},{9,... | collective-permute-start | bytes 110600 | tf_op jit(solution)/shard_map/ppermute | solution.py:747
  49.5 6.2 %collective-permute-start.30 = (f32[72,128]{1,0:T(8,128)S(1)}, f32[72,128]{1,0:T(8,128)S(1)}, u32[]{:S(2)}, u32[]{:S(2)}) collective-permute-start(f32[72,128]{1,0:T(8,128)S(1)} %add_add_fusion.1), channel_id=1, source_target_pairs={{0,8},{1,9},{2,10},{3,11},{4,12},{5,13},{6,14},{7,15},{8,0},{9,1},... | collective-permute-start | bytes 110600 | tf_op jit(solution)/shard_map/ppermute | solution.py:747
  55.7 1.3 %collective-permute-start.33 = (f32[72,128]{1,0:T(8,128)S(1)}, f32[72,128]{1,0:T(8,128)S(1)}, u32[]{:S(2)}, u32[]{:S(2)}) collective-permute-start(f32[72,128]{1,0:T(8,128)S(1)} %add_add_fusion.mine), channel_id=1, source_target_pairs={{0,1},{1,0},{2,3},{3,2},{4,5},{5,4},{6,7},{7,6},{8,9},{9,8},{10,11... | collective-permute-start | bytes 110600 | tf_op jit(solution)/shard_map/ppermute | solution.py:747
